TPU v7x, 32 devices: a whole 2x2x4 slice. The times are simulated.
32 devices in a mesh: lon: 8 (over y, x, core), lat: 4 (over z).
Axes of the slice: x: 2, y: 2, z: 4, core: 2. Of those that a mesh axis runs over, the one named last changes fastest.
Arguments:
- winds: bfloat16 [2, 32, 4, 384, 512], P(None, None, None, 'lon', 'lat'), may hold values from -60 to 60
Outputs:
- basis: float32 [48, 2, 4, 384, 512], P(None, None, None, 'lon', 'lat')
All inputs are finite; a program needn't handle non-finite values.
Results may differ from a plain program's by a relative error of at most 0.0043.
Values may be sent and summed in bfloat16 or wider, within the bound.
A program may use at most 128 MiB of HBM per device.

v0:
```python
import math

import jax
import jax.numpy as jnp
from jax import lax
from jax.sharding import PartitionSpec as P

TIME = 32
TAPERS = 12
FREQS = 2


def with_halo(cells, sides, width, closed):
    for axis, dim in sides:
        count = lax.axis_size(axis)
        ends = count if closed else count - 1
        head = lax.slice_in_dim(cells, 0, width, axis=dim)
        tail = lax.slice_in_dim(cells, cells.shape[dim] - width, cells.shape[dim], axis=dim)
        cells = jnp.concatenate(
            [
                lax.ppermute(tail, axis, [(i, (i + 1) % count) for i in range(ends)]),
                cells,
                lax.ppermute(head, axis, [((i + 1) % count, i) for i in range(ends)]),
            ],
            axis=dim,
        )
    return cells


def taper_table(times, tapers, freqs):
    times_f = jnp.arange(times, dtype=jnp.float32)
    order_k = jnp.arange(tapers, dtype=jnp.float32)
    weights = math.sqrt(2.0 / (times + 1)) * jnp.sin(
        math.pi * (order_k[:, None] + 1.0) * (times_f[None, :] + 1.0) / (times + 1)
    )
    blocks = []
    for which in range(freqs):
        phases = 2.0 * math.pi * (7 + 2 * which) * times_f / times
        real_part = weights * jnp.cos(phases)[None, :]
        imag_part = -weights * jnp.sin(phases)[None, :]
        blocks.append(jnp.stack([real_part, imag_part], axis=1).reshape(2 * tapers, times))
    return jnp.concatenate(blocks, axis=0).astype(jnp.bfloat16)


def stencil(lon_pad, lat_pad, cos_lat, step_lon, step_lat):
    along_lon = (
        lon_pad[..., 2:, :].astype(jnp.float32) - lon_pad[..., :-2, :].astype(jnp.float32)
    ) / (2.0 * step_lon)
    fluxes = lat_pad.astype(jnp.float32) * cos_lat
    along_lat = (fluxes[..., 2:] - fluxes[..., :-2]) / (2.0 * step_lat)
    middle = cos_lat[1:-1]
    vorticity = ((along_lon[1] - along_lat[0]) / middle).astype(jnp.bfloat16)
    divergence = ((along_lon[0] + along_lat[1]) / middle).astype(jnp.bfloat16)
    return (vorticity, divergence)


def body(winds):
    lon_cells = winds.shape[3]
    lat_cells = winds.shape[4]
    levels = winds.shape[2]
    times = winds.shape[1]
    grid_lon = lon_cells * lax.axis_size("lon")
    grid_lat = lat_cells * lax.axis_size("lat")
    step_lon = 2.0 * math.pi / grid_lon
    step_lat = 2.6 / grid_lat
    lon_pad = with_halo(winds, (("lon", 3),), 1, True)
    lat_pad = with_halo(winds, (("lat", 4),), 1, False)
    lat_index = lax.axis_index("lat") * lat_cells + jnp.arange(lat_cells + 2, dtype=jnp.int32) - 1
    lat_rows = lat_index.astype(jnp.float32)
    inside = jnp.logical_and(lat_index >= 0, lat_index < grid_lat)
    cos_plain = jnp.cos(-1.3 + (lat_rows + 0.5) * step_lat)
    cos_lat = jnp.where(inside, cos_plain, jnp.zeros_like(cos_plain))
    cos_lat = cos_lat.at[1:-1].set(cos_plain[1:-1])
    vorticity, divergence = stencil(lon_pad, lat_pad, cos_lat, step_lon, step_lat)
    table = taper_table(TIME, TAPERS, FREQS)
    vort_cols = jnp.dot(table, vorticity.reshape(times, -1), preferred_element_type=jnp.float32)
    div_cols = jnp.dot(table, divergence.reshape(times, -1), preferred_element_type=jnp.float32)
    snapshots = jnp.concatenate([vort_cols, div_cols], axis=1)
    columns = snapshots.reshape(FREQS, 2 * TAPERS, -1)
    total_rows = 2 * levels * grid_lon * grid_lat
    local_gram = (
        jnp.einsum("far,fbr->fab", columns, columns, precision=lax.Precision.HIGHEST) / total_rows
    )
    factor = jnp.linalg.cholesky(lax.psum(local_gram, ("lon", "lat")))
    basis = jax.scipy.linalg.solve_triangular(factor, columns, lower=True)
    return basis.reshape(2 * FREQS * TAPERS, 2, levels, lon_cells, lat_cells)


def solution(mesh):
    in_specs = (P(None, None, None, "lon", "lat"),)
    out_specs = P(None, None, None, "lon", "lat")
    return jax.shard_map(body, mesh=mesh, in_specs=in_specs, out_specs=out_specs, check_vma=False)
```

profile of v0, /device:TPU:0, one launch (start us, length us, event | category | flops | bytes accessed | tf_op | source)
XLA Modules:
  0.0 163.1 jit_solution(3344289362641082808)
XLA Ops:
  0.0 7.0 %fusion.13 = (bf16[2,32,4,48,1]{4,3,2,1,0:T(8,128)(2,1)}, bf16[2,32,4,48,1]{4,3,2,1,0:T(8,128)(2,1)}) fusion(bf16[2,32,4,48,128]{4,3,2,1,0:T(8,128)(2,1)} %param.3), kind=kLoop, calls=%fused_computation.49 | loop fusion | bytes 98304 | tf_op jit(solution)/shard_map/slice | solution.py:18
  7.0 4.6 %copy.21 = bf16[2,32,4,48,1]{3,1,4,2,0:T(8,128)(2,1)} copy(bf16[2,32,4,48,1]{4,3,2,1,0:T(8,128)(2,1)} %get-tuple-element.21) | data formatting | bytes 49152
  11.6 5.5 %collective-permute-start.2 = (bf16[2,32,4,48,1]{3,1,4,2,0:T(8,128)(2,1)}, bf16[2,32,4,48,1]{3,1,4,2,0:T(8,128)(2,1)}, u32[]{:S(2)}, u32[]{:S(2)}) collective-permute-start(bf16[2,32,4,48,1]{3,1,4,2,0:T(8,128)(2,1)} %copy.21), channel_id=1, source_target_pairs={{0,1},{1,2},{2,3},{4,5},{5,6},{6,7},{8,9},{9,10},{10,11},{12,13},{... | collective-permute-start | bytes 73736 | tf_op jit(solution)/shard_map/ppermute | solution.py:21
  17.1 4.4 %copy.22 = bf16[2,32,4,48,1]{3,1,4,2,0:T(8,128)(2,1)} copy(bf16[2,32,4,48,1]{4,3,2,1,0:T(8,128)(2,1)} %get-tuple-element.22) | data formatting | bytes 49152
  23.7 1.6 collective-permute-start
  27.7 1.4 fusion.14
  30.6 4.2 %copy.14 = bf16[2,32,4,48,1]{4,3,2,1,0:T(8,128)(2,1)} copy(bf16[2,32,4,48,1]{3,1,4,2,0:T(8,128)(2,1)} %collective-permute-done.2) | data formatting | bytes 49152 | tf_op jit(solution)/shard_map/ppermute | solution.py:21
  34.8 4.1 %copy.15 = bf16[2,32,4,48,1]{4,3,2,1,0:T(8,128)(2,1)} copy(bf16[2,32,4,48,1]{3,1,4,2,0:T(8,128)(2,1)} %collective-permute-done.3) | data formatting | bytes 49152 | tf_op jit(solution)/shard_map/ppermute | solution.py:23
  38.9 9.9 %convert_multiply_fusion = f32[2,32,4,48,130]{4,3,2,1,0:T(8,128)} fusion(bf16[2,32,4,48,1]{4,3,2,1,0:T(8,128)(2,1)} %copy.15, bf16[2,32,4,48,128]{4,3,2,1,0:T(8,128)(2,1)S(1)} %copy-done.1, bf16[2,32,4,48,1]{4,3,2,1,0:T(8,128)(2,1)} %copy.14, f32[130]{0:T(256)} %get-tuple-element.28), kind=kLoop, calls=%fused_computation | loop fusion | flops 11182080 | bytes 9585160 | tf_op jit(solution)/shard_map/mul | solution.py:49
  48.8 10.9 %fusion = f32[2,32,4,48,128]{4,3,2,1,0:T(8,128)} fusion(f32[2,32,4,48,130]{4,3,2,1,0:T(8,128)} %convert_multiply_fusion), kind=kLoop, calls=%fused_computation.3 | loop fusion | flops 3145728 | bytes 18874368 | tf_op jit(solution)/shard_map/div | solution.py:50
  59.7 3.8 %subtract_multiply_fusion = f32[2,32,4,48,128]{4,3,2,1,0:T(8,128)S(1)} fusion(bf16[2,32,4,48,128]{4,3,2,1,0:T(8,128)(2,1)S(1)} %copy-done.1, bf16[2,32,4,1,128]{4,3,2,1,0:T(2,128)(2,1)S(1)} %collective-permute-done.1, bf16[2,32,4,1,128]{4,3,2,1,0:T(2,128)(2,1)S(1)} %collective-permute-done), kind=kLoop, calls=%fused_computation.4 | loop fusion | flops 15728640 | bytes 9568256 | tf_op jit(solution)/shard_map/div | solution.py:46
  63.5 2.9 %slice_subtract_fusion.1 = (f32[1,32,4,48,128]{4,3,2,1,0:T(8,128)}, f32[1,32,4,48,128]{4,3,2,1,0:T(8,128)S(1)}) fusion(f32[2,32,4,48,128]{4,3,2,1,0:T(8,128)S(1)} %copy-done.2, f32[2,32,4,48,128]{4,3,2,1,0:T(8,128)S(1)} %subtract_multiply_fusion), kind=kLoop, calls=%fused_computation.6 | loop fusion | flops 1572864 | bytes 18874368 | tf_op jit(solution)/shard_map/sub | solution.py:52
  66.4 3.3 %sub.21 = f32[32,24576]{1,0:T(8,128)} reshape(f32[1,32,4,48,128]{4,3,2,1,0:T(8,128)} %get-tuple-element.17) | data formatting | bytes 6291456 | tf_op jit(solution)/shard_map/sub | solution.py:52
  69.7 1.9 %add.83 = f32[32,24576]{1,0:T(8,128)} reshape(f32[1,32,4,48,128]{4,3,2,1,0:T(8,128)S(1)} %get-tuple-element.18) | data formatting | bytes 6291456 | tf_op jit(solution)/shard_map/add | solution.py:53
  71.7 5.0 %fusion.1 = f32[48,24576]{1,0:T(8,128)} fusion(f32[32,24576]{1,0:T(8,128)} %sub.21, f32[24576]{0:T(1024)S(1)} %bitcast.27, bf16[24,32]{1,0:T(8,128)(2,1)S(1)} %bitcast.31, bf16[24,32]{1,0:T(8,128)(2,1)S(1)} %bitcast.29), kind=kOutput, calls=%fused_computation.11 | convolution fusion | flops 77076480 | bytes 7965696 | tf_op jit(solution)/shard_map/dot_general | solution.py:76
  76.7 2.9 %fusion.2 = f32[48,24576]{1,0:T(8,128)} fusion(f32[32,24576]{1,0:T(8,128)S(1)} %copy-done.3, f32[24576]{0:T(1024)S(1)} %bitcast.28, bf16[24,32]{1,0:T(8,128)(2,1)S(1)} %bitcast.32, bf16[24,32]{1,0:T(8,128)(2,1)S(1)} %bitcast.30), kind=kOutput, calls=%fused_computation.12 | convolution fusion | flops 77076480 | bytes 7965696 | tf_op jit(solution)/shard_map/dot_general | solution.py:77
  79.6 4.4 %pad_maximum_fusion = f32[48,49152]{1,0:T(8,128)S(1)} fusion(f32[48,24576]{1,0:T(8,128)} %fusion.2, f32[48,24576]{1,0:T(8,128)} %fusion.1), kind=kLoop, calls=%fused_computation.1 | loop fusion | flops 2359296 | bytes 18874368 | tf_op jit(solution)/shard_map/concatenate | solution.py:78
  84.0 3.7 %copy-done = f32[48,49152]{1,0:T(8,128)} copy-done((f32[48,49152]{1,0:T(8,128)}, f32[48,49152]{1,0:T(8,128)S(1)}, u32[]{:S(2)}) %copy-start) | copy-done | bytes 9437208
  87.7 9.9 %convolution_multiply_fusion = f32[2,24,24]{1,2,0:T(8,128)S(1)} fusion(f32[2,24,49152]{2,1,0:T(8,128)S(1)} %bitcast.24), kind=kOutput, calls=%fused_computation.15 | convolution fusion | flops 679478400 | bytes 9441792 | tf_op jit(solution)/shard_map/far,fbr->fab/dot_general | solution.py:82
  97.6 40.6 %psum.7 = f32[2,24,24]{1,2,0:T(8,128)S(1)} all-reduce(f32[2,24,24]{1,2,0:T(8,128)S(1)} %convolution_multiply_fusion), channel_id=1, replica_groups=mesh['lon'=8,'lat'=4] {'lon','lat'}, use_global_device_ids=true, to_apply=%region_0.1 | all-reduce | flops 1152 | bytes 9216 | tf_op jit(solution)/shard_map/psum | solution.py:84
  138.3 4.4 %custom-call.8 = f32[2,24,24]{2,1,0:T(8,128)S(1)} custom-call(f32[2,24,24]{2,1,0:T(8,128)S(1)} %fusion.7), custom_call_target="Cholesky" | custom-call | tf_op jit(solution)/shard_map/jit(cholesky)/cholesky | solution.py:84
  142.9 3.7 %custom-call.9 = f32[2,1,24,24]{2,3,1,0:T(8,128)S(1)} custom-call(f32[2,1,24,24]{3,2,1,0:T(8,128)S(1)} %select_bitcast_fusion), custom_call_target="InvertDiagBlocksLowerTriangular" | custom-call | tf_op jit(solution)/shard_map/jit(_solve_triangular)/vmap()/triangular_solve | solution.py:85
  146.6 11.1 %fusion.5 = f32[2,24,49152]{2,1,0:T(8,128)S(1)} fusion(f32[2,24,49152]{2,1,0:T(8,128)} %bitcast.25, f32[2,1,24,24]{2,3,1,0:T(8,128)S(1)} %custom-call.9), kind=kOutput, calls=%fused_computation.16 | convolution fusion | flops 679477248 | bytes 18878976 | tf_op jit(solution)/shard_map/jit(_solve_triangular)/vmap()/triangular_solve | solution.py:85
  157.8 5.4 %copy.23 = f32[6,8,384,128]{3,2,1,0:T(8,128)} copy(f32[6,8,384,128]{3,1,2,0:T(8,128)S(1)} %bitcast.26) | data formatting | bytes 18874368
  (35 shorter events, 6.4 us)
Async XLA Ops:
  7.0 15.9 %copy-start.1 = (bf16[2,32,4,48,128]{4,3,2,1,0:T(8,128)(2,1)S(1)}, bf16[2,32,4,48,128]{4,3,2,1,0:T(8,128)(2,1)}, u32[]{:S(2)}) copy-start(bf16[2,32,4,48,128]{4,3,2,1,0:T(8,128)(2,1)} %param.3) | copy-start | bytes 9437188
  11.6 19.0 %collective-permute-start.2 = (bf16[2,32,4,48,1]{3,1,4,2,0:T(8,128)(2,1)}, bf16[2,32,4,48,1]{3,1,4,2,0:T(8,128)(2,1)}, u32[]{:S(2)}, u32[]{:S(2)}) collective-permute-start(bf16[2,32,4,48,1]{3,1,4,2,0:T(8,128)(2,1)} %copy.21), channel_id=1, source_target_pairs={{0,1},{1,2},{2,3},{4,5},{5,6},{6,7},{8,9},{9,10},{10,11},{12,13},{... | collective-permute-start | bytes 73736 | tf_op jit(solution)/shard_map/ppermute | solution.py:21
  21.6 13.3 %collective-permute-start.3 = (bf16[2,32,4,48,1]{3,1,4,2,0:T(8,128)(2,1)}, bf16[2,32,4,48,1]{3,1,4,2,0:T(8,128)(2,1)}, u32[]{:S(2)}, u32[]{:S(2)}) collective-permute-start(bf16[2,32,4,48,1]{3,1,4,2,0:T(8,128)(2,1)} %copy.22), channel_id=1, source_target_pairs={{1,0},{2,1},{3,2},{5,4},{6,5},{7,6},{9,8},{10,9},{11,10},{13,12},{... | collective-permute-start | bytes 73736 | tf_op jit(solution)/shard_map/ppermute | solution.py:23
  23.7 35.9 %collective-permute-start = (bf16[2,32,4,1,128]{4,3,2,1,0:T(2,128)(2,1)}, bf16[2,32,4,1,128]{4,3,2,1,0:T(2,128)(2,1)S(1)}, u32[]{:S(2)}, u32[]{:S(2)}) collective-permute-start(bf16[2,32,4,1,128]{4,3,2,1,0:T(2,128)(2,1)} %get-tuple-element.19), channel_id=1, source_target_pairs={{4,0},{8,4},{12,8},{16,12},{20,16},{24,20},{28,24},{0,28},{5,1},{9... | collective-permute-start | bytes 196616 | tf_op jit(solution)/shard_map/ppermute | solution.py:23
  25.3 34.3 %collective-permute-start.1 = (bf16[2,32,4,1,128]{4,3,2,1,0:T(2,128)(2,1)S(1)}, bf16[2,32,4,1,128]{4,3,2,1,0:T(2,128)(2,1)S(1)}, u32[]{:S(2)}, u32[]{:S(2)}) collective-permute-start(bf16[2,32,4,1,128]{4,3,2,1,0:T(2,128)(2,1)S(1)} %get-tuple-element.20), channel_id=1, source_target_pairs={{0,4},{4,8},{8,12},{12,16},{16,20},{20,24},{24,28},{28,0},{1,5},{5... | collective-permute-start | bytes 196616 | tf_op jit(solution)/shard_map/ppermute | solution.py:21
  59.6 3.8 %copy-start.2 = (f32[2,32,4,48,128]{4,3,2,1,0:T(8,128)S(1)}, f32[2,32,4,48,128]{4,3,2,1,0:T(8,128)}, u32[]{:S(2)}) copy-start(f32[2,32,4,48,128]{4,3,2,1,0:T(8,128)} %fusion) | copy-start | bytes 18874372
  66.4 5.3 %copy-start.5 = (f32[128]{0:T(128)S(1)}, f32[128]{0:T(128)}, u32[]{:S(2)}) copy-start(f32[128]{0:T(128)} %get-tuple-element.27) | copy-start | bytes 1540
  66.4 5.3 %copy-start.4 = (bf16[12,2,32]{2,1,0:T(2,128)(2,1)S(1)}, bf16[12,2,32]{2,1,0:T(2,128)(2,1)}, u32[]{:S(2)}) copy-start(bf16[12,2,32]{2,1,0:T(2,128)(2,1)} %get-tuple-element.32) | copy-start | bytes 4612
  71.7 5.0 %copy-start.3 = (f32[32,24576]{1,0:T(8,128)S(1)}, f32[32,24576]{1,0:T(8,128)}, u32[]{:S(2)}) copy-start(f32[32,24576]{1,0:T(8,128)} %add.83) | copy-start | bytes 9437188
  84.0 3.7 %copy-start = (f32[48,49152]{1,0:T(8,128)}, f32[48,49152]{1,0:T(8,128)S(1)}, u32[]{:S(2)}) copy-start(f32[48,49152]{1,0:T(8,128)S(1)} %pad_maximum_fusion) | copy-start | bytes 28311556
where the time goes:
time: 164 us; the launch traced here: 163 us
  other arithmetic  44 us (27%)
  local copies, waits for them, and re-layouts  41 us (25%)
  blocking collectives  40.6 us (25%)
  matrix products  28.9 us (18%)
  starting transfers between devices  8.44 us (5%)
    psum x1, blocking collectives, body(): factor = jnp.linalg.cholesky(lax.psum(local_gram, ('lon', 'lat')))  40.6 us
    unnamed x15, local copies, waits for them, and re-layouts  18.1 us
    another operation x1, matrix products, body(): basis = jax.scipy.linalg.solve_triangular(factor, columns, lower=True)  11.1 us
    div x1, other arithmetic, stencil(): along_lat = (fluxes[..., 2:] - fluxes[..., :-2]) / (2.0 * step_lat)  10.9 us
    dot_general x1, matrix products, body(): jnp.einsum('far,fbr->fab', columns, columns, precision=lax.Precision.HIGH...  9.88 us
    mul x1, other arithmetic, stencil(): fluxes = lat_pad.astype(jnp.float32) * cos_lat  9.86 us
    slice x1, local copies, waits for them, and re-layouts, with_halo(): lax.slice_in_dim(cells, cells.shape[dim] - width, cells.shape[dim], axis=...  6.98 us
    ppermute x2, starting transfers between devices, with_halo(): lax.ppermute(tail, axis, [(i, (i + 1) % count) for i in range(ends)])  5.55 us
  transfers between devices with their start and end apart: 4, of which 0 were waited for; matrix products, arithmetic and copies ran while one was open for 24% of the time, Pallas kernels for 0%

commit v1 on v0

v1 whole, which is shorter than its diff:
```python
import functools
import math

import jax
import jax.numpy as jnp
import ml_dtypes
import numpy as np
from jax import lax
from jax.experimental import pallas as pl
from jax.experimental.pallas import tpu as pltpu
from jax.sharding import PartitionSpec as P

TIME = 32
TAPERS = 12
FREQS = 2
COLS = 2 * TAPERS
ALL = FREQS * COLS
SUB = 8
LANES = 128
PITCH = 64
LEAD = 8
CHUNKS = 4
MESH = pl.DeviceIdType.MESH
F32 = jnp.float32
BF16 = jnp.bfloat16


def taper_table():
    t = np.arange(TIME, dtype=np.float64)
    k = np.arange(TAPERS, dtype=np.float64)
    weights = math.sqrt(2.0 / (TIME + 1)) * np.sin(
        math.pi * (k[:, None] + 1.0) * (t[None, :] + 1.0) / (TIME + 1)
    )
    blocks = []
    for which in range(FREQS):
        phases = 2.0 * math.pi * (7 + 2 * which) * t / TIME
        pair = np.stack([weights * np.cos(phases), -weights * np.sin(phases)], axis=1)
        blocks.append(pair.reshape(COLS, TIME))
    return np.concatenate(blocks, axis=0).astype(np.float32).astype(ml_dtypes.bfloat16)


def lat_coefficients(grid_lon, grid_lat, bands):
    step_lon = 2.0 * math.pi / grid_lon
    step_lat = 2.6 / grid_lat
    cos_lat = np.cos(-1.3 + (np.arange(-1, grid_lat + 1) + 0.5) * step_lat)
    middle = cos_lat[1:-1]
    rows = np.stack(
        [
            1.0 / (2.0 * step_lon * middle),
            cos_lat[2:] / (2.0 * step_lat * middle),
            cos_lat[:-2] / (2.0 * step_lat * middle),
        ]
    ).astype(np.float32)
    rows = rows.reshape(3, bands, 1, LANES).transpose(1, 0, 2, 3)
    return np.broadcast_to(rows, (bands, 3, SUB, LANES)).copy()


def split(value, parts):
    pieces = []
    for _ in range(parts):
        piece = value.astype(BF16)
        pieces.append(piece)
        value = value - piece.astype(F32)
    return pieces


def iota(shape, dim):
    return lax.broadcasted_iota(jnp.int32, shape, dim)


def dot(a, b):
    return jnp.dot(a, b, preferred_element_type=F32)


def fields_kernel(
    n_lon, n_lat, levels, lon_cells, rows_total,
    winds, coef, table3, table_t, table_aug,
    x_out, mix_out,
    raw, padded, x_buf, pbuf, from_left, from_right, edges, row_first, row_last,
    row_prev, row_next, gram, mine, lon_slots, band, lat_slots,
    in_sem, out_sem, halo_send, halo_recv, lon_send, lon_recv, lat_send, lat_recv,
):
    lon = lax.axis_index("lon")
    lat = lax.axis_index("lat")
    groups = lon_cells // SUB
    blocks = 2 * TIME * levels
    per = 2 * TIME // CHUNKS
    cells = levels * lon_cells

    def load(c):
        part = pl.ds(c * per, per)
        return pltpu.make_async_copy(winds.at[part], raw.at[part], in_sem.at[c])

    for c in range(CHUNKS):
        load(c).start()
    from_left[...] = jnp.zeros_like(from_left)
    from_right[...] = jnp.zeros_like(from_right)

    barrier = pltpu.get_barrier_semaphore()
    for d in range(1, n_lon):
        pl.semaphore_signal(
            barrier, inc=1, device_id=(lax.rem(lon + d, n_lon), lat), device_id_type=MESH
        )
    for d in range(1, n_lat):
        pl.semaphore_signal(
            barrier, inc=1, device_id=(lon, lax.rem(lat + d, n_lat)), device_id_type=MESH
        )

    lane_c = iota((cells, LANES), 1)

    def widen(q, packed):
        x = raw[q].astype(F32)
        for l in range(levels):
            start = pl.multiple_of((q * levels + l) * PITCH + LEAD, 8)
            padded[pl.ds(start, lon_cells), :] = x[l * lon_cells:(l + 1) * lon_cells]
        turned = pltpu.roll(x, 2 * q + 1, 1)
        return jnp.where(lane_c // 2 == q, turned, packed)

    packed = jnp.zeros((cells, LANES), F32)
    for c in range(CHUNKS):
        load(c).wait()
        packed = lax.fori_loop(c * per, (c + 1) * per, widen, packed)
    pbuf[...] = packed.astype(BF16)

    pl.semaphore_wait(barrier, n_lon + n_lat - 2)

    def remote(src, dst, send, recv, device):
        return pltpu.make_async_remote_copy(
            src_ref=src, dst_ref=dst, send_sem=send, recv_sem=recv,
            device_id=device, device_id_type=MESH,
        )

    up = remote(pbuf, from_left, halo_send.at[0], halo_recv.at[0], (lon, lax.rem(lat + 1, n_lat)))
    down = remote(
        pbuf, from_right, halo_send.at[1], halo_recv.at[1], (lon, lax.rem(lat + n_lat - 1, n_lat))
    )
    pl.when(lat < n_lat - 1)(lambda: up.start())
    pl.when(lat > 0)(lambda: down.start())

    row_first[...] = padded[pl.ds(LEAD, blocks, stride=PITCH), :].astype(BF16)
    row_last[...] = padded[pl.ds(LEAD + lon_cells - 1, blocks, stride=PITCH), :].astype(BF16)
    east = remote(
        row_last, row_prev, halo_send.at[2], halo_recv.at[2], (lax.rem(lon + 1, n_lon), lat)
    )
    west = remote(
        row_first, row_next, halo_send.at[3], halo_recv.at[3], (lax.rem(lon + n_lon - 1, n_lon), lat)
    )
    east.start()
    west.start()

    pl.when(lat > 0)(lambda: up.wait_recv())
    pl.when(lat < n_lat - 1)(lambda: down.wait_recv())
    edges[...] = jnp.where(
        lane_c % 2 == 0,
        from_left[...].astype(F32),
        pltpu.roll(from_right[...].astype(F32), LANES - 2, 1),
    )
    east.wait_recv()
    padded[pl.ds(LEAD - 1, blocks, stride=PITCH), :] = row_prev[...].astype(F32)
    west.wait_recv()
    padded[pl.ds(LEAD + lon_cells, blocks, stride=PITCH), :] = row_next[...].astype(F32)

    batch = 4
    lane = iota((batch * SUB, LANES), 1)
    first = lane == 0
    last = lane == LANES - 1
    along = jnp.concatenate([coef[lat, 0]] * batch, axis=0)
    ahead = jnp.concatenate([coef[lat, 1]] * batch, axis=0)
    behind = jnp.concatenate([coef[lat, 2]] * batch, axis=0)

    def one_group(step, carry):
        level = step // groups
        group = lax.rem(step, groups)
        edge = edges[pl.ds(pl.multiple_of(step * SUB, SUB), SUB), :]
        for t0 in range(0, TIME, batch):
            d_lon, d_lat = [], []
            for comp in range(2):
                def rows(shift):
                    parts = []
                    for t in range(t0, t0 + batch):
                        q = comp * TIME + t
                        start = (q * levels + level) * PITCH + LEAD + group * SUB + shift
                        parts.append(padded[pl.ds(start, SUB), :])
                    return jnp.concatenate(parts, axis=0)

                d_lon.append((rows(1) - rows(-1)) * along)
                center = rows(0)
                halo = jnp.concatenate(
                    [
                        pltpu.roll(edge, (LANES - 2 * (comp * TIME + t)) % LANES, 1)
                        for t in range(t0, t0 + batch)
                    ],
                    axis=0,
                )
                nxt = jnp.where(last, halo, pltpu.roll(center, LANES - 1, 1))
                prv = jnp.where(first, halo, pltpu.roll(center, 1, 1))
                d_lat.append(nxt * ahead - prv * behind)
            here = pl.ds(t0 * SUB, batch * SUB)
            vort_at = pl.ds(pl.multiple_of(step * LANES, LANES), LANES)
            div_at = pl.ds(pl.multiple_of((step + levels * groups) * LANES, LANES), LANES)
            x_buf[here, vort_at] = (d_lon[1] - d_lat[0]).astype(BF16)
            x_buf[here, div_at] = (d_lon[0] + d_lat[1]).astype(BF16)
        return carry

    lax.fori_loop(0, levels * groups, one_group, 0)
    store = pltpu.make_async_copy(x_buf, x_out, out_sem)
    store.start()

    wide = 8 * LANES
    side = TIME * SUB

    def add_gram(c, carry):
        x = x_buf[:, pl.ds(pl.multiple_of(c * wide, wide), wide)]
        term = lax.dot_general(x, x, (((1,), (1,)), ((), ())), preferred_element_type=F32)
        gram[...] = gram[...] + term
        return carry

    gram[...] = jnp.zeros_like(gram)
    lax.fori_loop(0, 2 * levels * groups * LANES // wide, add_gram, 0)
    same = iota((side, side), 0) % SUB == iota((side, side), 1) % SUB
    by_time = jnp.sum(jnp.where(same, gram[...], 0.0).reshape(TIME, SUB, side), axis=1)
    fold = (iota((side, LANES), 0) // SUB == iota((side, LANES), 1)).astype(F32).astype(BF16)
    folded = dot(jnp.concatenate(split(by_time, 3), axis=0), fold)
    times = folded[:TIME] + folded[TIME:2 * TIME] + folded[2 * TIME:]
    tile = times[:SUB]
    for a in range(1, TIME // SUB):
        tile = tile + pltpu.roll(times[a * SUB:(a + 1) * SUB], a * TIME, 1)
    mine[...] = tile

    lon_copies = [
        remote(mine, lon_slots.at[d - 1], lon_send.at[d - 1], lon_recv.at[d - 1],
               (lax.rem(lon + d, n_lon), lat))
        for d in range(1, n_lon)
    ]
    for copy in lon_copies:
        copy.start()
    total = mine[...]
    for d, copy in enumerate(lon_copies):
        copy.wait_recv()
        total = total + lon_slots[d]
    band[...] = total
    lat_copies = [
        remote(band, lat_slots.at[d - 1], lat_send.at[d - 1], lat_recv.at[d - 1],
               (lon, lax.rem(lat + d, n_lat)))
        for d in range(1, n_lat)
    ]
    for copy in lat_copies:
        copy.start()
    total = band[...]
    for d, copy in enumerate(lat_copies):
        copy.wait_recv()
        total = total + lat_slots[d]

    total = total * (1.0 / rows_total)
    square = jnp.concatenate(
        [total] + [pltpu.roll(total, LANES - a * TIME, 1) for a in range(1, TIME // SUB)], axis=0
    )
    half = dot(table3[...], jnp.concatenate(split(square, 3), axis=0))
    full = dot(jnp.concatenate(split(half, 3), axis=0), table_t[...])
    full = full[:ALL] + full[ALL:2 * ALL] + full[2 * ALL:]
    aug = jnp.where(iota((ALL, LANES), 1) < 64, full, table_aug[...])
    row = iota((COLS, 1), 0)
    lane_a = iota((COLS, LANES), 1)
    parts = [aug[:COLS], aug[COLS:]]
    for k in range(COLS):
        for f in range(FREQS):
            a = parts[f]
            at = f * COLS + k
            pivot = a[k:k + 1, :]
            scale = jnp.where(row > k, a[:, at:at + 1] / pivot[:, at:at + 1], 0.0)
            parts[f] = a - scale * pivot
    rows_done = []
    for f in range(FREQS):
        on_diag = lane_a == iota((COLS, LANES), 0) + f * COLS
        diag = jnp.sum(jnp.where(on_diag, parts[f], 0.0), axis=1, keepdims=True)
        rows_done.append(parts[f] / jnp.sqrt(diag))
    mix = jnp.concatenate(rows_done, axis=0)
    spread = (iota((LANES, side), 0) - 64 == iota((LANES, side), 1) // SUB).astype(F32).astype(BF16)
    wide_mix = dot(jnp.concatenate(split(mix, 2), axis=0), spread)
    tall = jnp.broadcast_to(wide_mix[:, None, :], (2 * ALL, SUB, side)).reshape(2 * ALL * SUB, side)
    keep = iota(tall.shape, 0) % SUB == iota(tall.shape, 1) % SUB
    tall = jnp.where(keep, tall, 0.0).astype(BF16)
    mix_out[:, :side] = tall[:ALL * SUB]
    mix_out[:, side:] = tall[ALL * SUB:]

    pl.when(lat < n_lat - 1)(lambda: up.wait_send())
    pl.when(lat > 0)(lambda: down.wait_send())
    for copy in [east, west] + lon_copies + lat_copies:
        copy.wait_send()
    store.wait()


def basis_kernel(mix, x, out):
    lon_cells = out.shape[2]
    weights = mix[...]
    for g in range(0, lon_cells // SUB, 2):
        part = x[:, g * LANES:(g + 2) * LANES]
        res = dot(weights, jnp.concatenate([part, part], axis=0))
        for h in range(2):
            cols = res[:, h * LANES:(h + 1) * LANES].reshape(ALL, SUB, LANES)
            out[:, 0, (g + h) * SUB:(g + h + 1) * SUB, :] = cols


def body(n_lon, n_lat, winds):
    _, times, levels, lon_cells, lat_cells = winds.shape
    cells = levels * lon_cells
    columns = 2 * cells // SUB * LANES
    side = TIME * SUB
    table = taper_table()
    table3 = np.concatenate([table] * 3, axis=1)
    table_t = np.zeros((LANES, LANES), ml_dtypes.bfloat16)
    table_t[:TIME, :ALL] = table.T
    table_aug = np.zeros((ALL, LANES), np.float32)
    table_aug[:, 64:64 + TIME] = table.astype(np.float32)
    coef = lat_coefficients(n_lon * lon_cells, n_lat * lat_cells, n_lat)
    rows_total = 2 * levels * lon_cells * n_lon * lat_cells * n_lat
    vmem = pl.BlockSpec(memory_space=pltpu.VMEM)
    anywhere = pl.BlockSpec(memory_space=pl.ANY)
    blocks = 2 * TIME * levels
    dma = pltpu.SemaphoreType.DMA
    x, mix = pl.pallas_call(
        functools.partial(fields_kernel, n_lon, n_lat, levels, lon_cells, rows_total),
        out_shape=(
            jax.ShapeDtypeStruct((side, columns), BF16),
            jax.ShapeDtypeStruct((ALL * SUB, 2 * side), BF16),
        ),
        in_specs=[anywhere, vmem, vmem, vmem, vmem],
        out_specs=(anywhere, vmem),
        scratch_shapes=[
            pltpu.VMEM((2 * TIME, cells, LANES), BF16),
            pltpu.VMEM((blocks * PITCH, LANES), F32),
            pltpu.VMEM((side, columns), BF16),
            pltpu.VMEM((cells, LANES), BF16),
            pltpu.VMEM((cells, LANES), BF16),
            pltpu.VMEM((cells, LANES), BF16),
            pltpu.VMEM((cells, LANES), F32),
            pltpu.VMEM((blocks, LANES), BF16),
            pltpu.VMEM((blocks, LANES), BF16),
            pltpu.VMEM((blocks, LANES), BF16),
            pltpu.VMEM((blocks, LANES), BF16),
            pltpu.VMEM((side, side), F32),
            pltpu.VMEM((SUB, LANES), F32),
            pltpu.VMEM((n_lon - 1, SUB, LANES), F32),
            pltpu.VMEM((SUB, LANES), F32),
            pltpu.VMEM((n_lat - 1, SUB, LANES), F32),
            dma((CHUNKS,)),
            dma(()),
            dma((4,)),
            dma((4,)),
            dma((n_lon - 1,)),
            dma((n_lon - 1,)),
            dma((n_lat - 1,)),
            dma((n_lat - 1,)),
        ],
        compiler_params=pltpu.CompilerParams(
            collective_id=0, has_side_effects=True, vmem_limit_bytes=40 * 2**20
        ),
        name="fields",
    )(
        winds.reshape(2 * TIME, cells, LANES),
        jnp.asarray(coef),
        jnp.asarray(table3),
        jnp.asarray(table_t),
        jnp.asarray(table_aug),
    )
    width = lon_cells // SUB * LANES
    basis = pl.pallas_call(
        basis_kernel,
        grid=(2 * levels,),
        out_shape=jax.ShapeDtypeStruct((ALL, 2 * levels, lon_cells, LANES), F32),
        in_specs=[
            pl.BlockSpec((ALL * SUB, 2 * side), lambda i: (0, 0)),
            pl.BlockSpec((side, width), lambda i: (0, i)),
        ],
        out_specs=pl.BlockSpec((ALL, 1, lon_cells, LANES), lambda i: (0, i, 0, 0)),
        compiler_params=pltpu.CompilerParams(vmem_limit_bytes=40 * 2**20),
        name="basis",
    )(mix, x)
    return basis.reshape(ALL, 2, levels, lon_cells, lat_cells)


def solution(mesh):
    spec = P(None, None, None, "lon", "lat")
    run = functools.partial(body, mesh.shape["lon"], mesh.shape["lat"])
    return jax.shard_map(run, mesh=mesh, in_specs=(spec,), out_specs=spec, check_vma=False)
```

time: 164 us -> 43.4 us (0.26)
  other arithmetic: 44 us -> 0 us
  blocking collectives: 40.6 us -> 0 us
  Pallas kernels: 0 us -> 38.1 us
  local copies, waits for them, and re-layouts: 41 us -> 4.89 us
  matrix products: 28.9 us -> 0 us
  starting transfers between devices: 8.44 us -> 0 us
    psum x1 -> x0, blocking collectives: 40.6 us -> none  [body(): factor = jnp.linalg.cholesky(lax.psum(local_gram, ('lon', 'lat')))]
    pallas_call x0 -> x2, Pallas kernels: none -> 38.1 us  [the longest x1 31.5 us: body(): pl.pallas_call(functools.partial(fields_kernel, n_lon, n_lat, levels, lon...]
    dot_general x3 -> x0, matrix products: 17.8 us -> none  [the longest x1 9.88 us: body(): jnp.einsum('far,fbr->fab', columns, columns, precision=lax.Precision.HIGH...]
    div x3 -> x0, other arithmetic: 14.7 us -> none  [the longest x1 10.9 us: stencil(): along_lat = (fluxes[..., 2:] - fluxes[..., :-2]) / (2.0 * step_lat)]
    unnamed x15 -> x10, local copies, waits for them, and re-layouts: 18.1 us -> 4.89 us
    another operation x1 -> x0, matrix products: 11.1 us -> none  [body(): basis = jax.scipy.linalg.solve_triangular(factor, columns, lower=True)]
    mul x4 -> x0, other arithmetic: 9.96 us -> none  [the longest x1 9.86 us: stencil(): fluxes = lat_pad.astype(jnp.float32) * cos_lat]
    another operation x9 -> x0, other arithmetic: 9.84 us -> none  [the longest x4 4.56 us: body(): factor = jnp.linalg.cholesky(lax.psum(local_gram, ('lon', 'lat')))]
  transfers between devices with their start and end apart: 4 -> 0, of which waited for: 0 -> 0; matrix products, arithmetic and copies ran while one was open for 24% -> 0% of each run, Pallas kernels for 0% -> 0%
where the time goes in v1:
time: 43.4 us; the launch traced here: 43 us
  Pallas kernels  38.1 us (88%)
  local copies, waits for them, and re-layouts  4.89 us (11%)
    pallas_call x1, Pallas kernels, body(): pl.pallas_call(functools.partial(fields_kernel, n_lon, n_lat, levels, lon...  31.5 us
    pallas_call x1, Pallas kernels, body(): pl.pallas_call(basis_kernel, grid=(2 * levels,), out_shape=jax.ShapeDtype...  6.59 us
    unnamed x10, local copies, waits for them, and re-layouts  4.89 us

profile of v1, /device:TPU:0, one launch (start us, length us, event | category | flops | bytes accessed | tf_op | source)
XLA Modules:
  0.0 43.0 jit_solution(12353397289763330802)
XLA Ops:
  0.0 0.0 copy-start
  0.0 1.9 %copy-done = bf16[2,32,4,48,128]{4,3,2,1,0:T(8,128)(2,1)S(1)} copy-done((bf16[2,32,4,48,128]{4,3,2,1,0:T(8,128)(2,1)S(1)}, bf16[2,32,4,48,128]{4,3,2,1,0:T(8,128)(2,1)}, u32[]{:S(2)}) %copy-start) | copy-done | bytes 3145752
  1.9 0.0 copy-start.1
  1.9 0.8 %copy-done.1 = f32[4,3,8,128]{3,2,1,0:T(8,128)S(1)} copy-done((f32[4,3,8,128]{3,2,1,0:T(8,128)S(1)}, f32[4,3,8,128]{3,2,1,0:T(8,128)}, u32[]{:S(2)}) %copy-start.1) | copy-done | bytes 49176
  2.7 0.0 copy-start.2
  2.7 0.8 %copy-done.2 = bf16[128,128]{1,0:T(8,128)(2,1)S(1)} copy-done((bf16[128,128]{1,0:T(8,128)(2,1)S(1)}, bf16[128,128]{1,0:T(8,128)(2,1)}, u32[]{:S(2)}) %copy-start.2) | copy-done | bytes 32792
  3.4 0.0 copy-start.3
  3.5 0.7 %copy-done.3 = f32[48,128]{1,0:T(8,128)S(1)} copy-done((f32[48,128]{1,0:T(8,128)S(1)}, f32[48,128]{1,0:T(8,128)}, u32[]{:S(2)}) %copy-start.3) | copy-done | bytes 24600
  4.2 0.0 copy-start.4
  4.2 0.7 %copy-done.4 = bf16[48,96]{1,0:T(8,128)(2,1)S(1)} copy-done((bf16[48,96]{1,0:T(8,128)(2,1)S(1)}, bf16[48,96]{1,0:T(8,128)(2,1)}, u32[]{:S(2)}) %copy-start.4) | copy-done | bytes 9240
  4.9 31.5 %fields.1 = (bf16[256,6144]{1,0:T(8,128)(2,1)S(1)}, bf16[384,512]{1,0:T(8,128)(2,1)S(1)}) custom-call(bf16[64,192,128]{2,1,0:T(8,128)(2,1)S(1)} %bitcast.2, f32[4,3,8,128]{3,2,1,0:T(8,128)S(1)} %copy-done.1, bf16[48,96]{1,0:T(8,128)(2,1)S(1)} %copy-done.4, bf16[128,128]{1,0:T(8,128)(2,1)S(1)} %copy-done.2, f32[48,128]{1,0:T(8,128)S(1)} %copy-done.3), custom_call_target="tpu_custom_call" | custom-call | tf_op jit(solution)/shard_map/fields/pallas_call | solution.py:321
  36.4 6.6 %basis.1 = f32[48,8,48,128]{3,2,1,0:T(8,128)} custom-call(bf16[384,512]{1,0:T(8,128)(2,1)S(1)} %get-tuple-element.7.mix, bf16[256,6144]{1,0:T(8,128)(2,1)S(1)} %get-tuple-element.8.x), custom_call_target="tpu_custom_call" | custom-call | tf_op jit(solution)/shard_map/basis/pallas_call | solution.py:367
Async XLA Ops:
  0.0 1.9 %copy-start = (bf16[2,32,4,48,128]{4,3,2,1,0:T(8,128)(2,1)S(1)}, bf16[2,32,4,48,128]{4,3,2,1,0:T(8,128)(2,1)}, u32[]{:S(2)}) copy-start(bf16[2,32,4,48,128]{4,3,2,1,0:T(8,128)(2,1)} %param.5) | copy-start | bytes 9437188
  1.9 0.8 %copy-start.1 = (f32[4,3,8,128]{3,2,1,0:T(8,128)S(1)}, f32[4,3,8,128]{3,2,1,0:T(8,128)}, u32[]{:S(2)}) copy-start(f32[4,3,8,128]{3,2,1,0:T(8,128)} %constant.8.clone.coef) | copy-start | bytes 147460
  2.7 0.8 %copy-start.2 = (bf16[128,128]{1,0:T(8,128)(2,1)S(1)}, bf16[128,128]{1,0:T(8,128)(2,1)}, u32[]{:S(2)}) copy-start(bf16[128,128]{1,0:T(8,128)(2,1)} %constant.10.clone.table_t) | copy-start | bytes 98308
  3.4 0.7 %copy-start.3 = (f32[48,128]{1,0:T(8,128)S(1)}, f32[48,128]{1,0:T(8,128)}, u32[]{:S(2)}) copy-start(f32[48,128]{1,0:T(8,128)} %constant.11.clone.table_aug) | copy-start | bytes 73732
  4.2 0.7 %copy-start.4 = (bf16[48,96]{1,0:T(8,128)(2,1)S(1)}, bf16[48,96]{1,0:T(8,128)(2,1)}, u32[]{:S(2)}) copy-start(bf16[48,96]{1,0:T(8,128)(2,1)} %constant.9.clone.table3) | copy-start | bytes 27652

commit v2 on v1

--- a/solution.py
+++ b/solution.py
@@ -17,7 +17,7 @@
 ALL = FREQS * COLS
 SUB = 8
 LANES = 128
-PITCH = 64
+PITCH = 56
 LEAD = 8
 CHUNKS = 4
 MESH = pl.DeviceIdType.MESH
@@ -74,11 +74,11 @@
 
 def fields_kernel(
     n_lon, n_lat, levels, lon_cells, rows_total,
-    winds, coef, table3, table_t, table_aug,
+    winds, consts,
     x_out, mix_out,
-    raw, padded, x_buf, pbuf, from_left, from_right, edges, row_first, row_last,
+    coef, tables, raw, padded, x_buf, pbuf, from_left, from_right, edges, row_first, row_last,
     row_prev, row_next, gram, mine, lon_slots, band, lat_slots,
-    in_sem, out_sem, halo_send, halo_recv, lon_send, lon_recv, lat_send, lat_recv,
+    in_sem, const_sem, out_sem, halo_send, halo_recv, lon_send, lon_recv, lat_send, lat_recv,
 ):
     lon = lax.axis_index("lon")
     lat = lax.axis_index("lat")
@@ -93,6 +93,15 @@
 
     for c in range(CHUNKS):
         load(c).start()
+    band_rows = 3 * SUB
+    get_coef = pltpu.make_async_copy(
+        consts.at[pl.ds(pl.multiple_of(lat * band_rows, 8), band_rows)], coef, const_sem.at[0]
+    )
+    get_tables = pltpu.make_async_copy(
+        consts.at[pl.ds(n_lat * band_rows, tables.shape[0])], tables, const_sem.at[1]
+    )
+    get_coef.start()
+    get_tables.start()
     from_left[...] = jnp.zeros_like(from_left)
     from_right[...] = jnp.zeros_like(from_right)
 
@@ -106,21 +115,21 @@
             barrier, inc=1, device_id=(lon, lax.rem(lat + d, n_lat)), device_id_type=MESH
         )
 
-    lane_c = iota((cells, LANES), 1)
+    pair = iota((SUB, LANES), 1) >> 1
 
     def widen(q, packed):
         x = raw[q].astype(F32)
         for l in range(levels):
             start = pl.multiple_of((q * levels + l) * PITCH + LEAD, 8)
             padded[pl.ds(start, lon_cells), :] = x[l * lon_cells:(l + 1) * lon_cells]
-        turned = pltpu.roll(x, 2 * q + 1, 1)
-        return jnp.where(lane_c // 2 == q, turned, packed)
-
-    packed = jnp.zeros((cells, LANES), F32)
+        turned = pltpu.roll(x, 2 * q + 1, 1).reshape(cells // SUB, SUB, LANES)
+        return jnp.where((pair == q)[None], turned, packed)
+
+    packed = jnp.zeros((cells // SUB, SUB, LANES), F32)
     for c in range(CHUNKS):
         load(c).wait()
         packed = lax.fori_loop(c * per, (c + 1) * per, widen, packed)
-    pbuf[...] = packed.astype(BF16)
+    pbuf[...] = packed.reshape(cells, LANES).astype(BF16)
 
     pl.semaphore_wait(barrier, n_lon + n_lat - 2)
 
@@ -151,7 +160,7 @@
     pl.when(lat > 0)(lambda: up.wait_recv())
     pl.when(lat < n_lat - 1)(lambda: down.wait_recv())
     edges[...] = jnp.where(
-        lane_c % 2 == 0,
+        iota((cells, LANES), 1) % 2 == 0,
         from_left[...].astype(F32),
         pltpu.roll(from_right[...].astype(F32), LANES - 2, 1),
     )
@@ -164,13 +173,14 @@
     lane = iota((batch * SUB, LANES), 1)
     first = lane == 0
     last = lane == LANES - 1
-    along = jnp.concatenate([coef[lat, 0]] * batch, axis=0)
-    ahead = jnp.concatenate([coef[lat, 1]] * batch, axis=0)
-    behind = jnp.concatenate([coef[lat, 2]] * batch, axis=0)
-
-    def one_group(step, carry):
-        level = step // groups
-        group = lax.rem(step, groups)
+    get_coef.wait()
+    along, ahead, behind = (
+        jnp.concatenate([coef[i * SUB:(i + 1) * SUB, :]] * batch, axis=0) for i in range(3)
+    )
+
+    def one_group(level, group):
+        step = level * groups + group
+        base = level * PITCH + group * SUB
         edge = edges[pl.ds(pl.multiple_of(step * SUB, SUB), SUB), :]
         for t0 in range(0, TIME, batch):
             d_lon, d_lat = [], []
@@ -178,9 +188,8 @@
                 def rows(shift):
                     parts = []
                     for t in range(t0, t0 + batch):
-                        q = comp * TIME + t
-                        start = (q * levels + level) * PITCH + LEAD + group * SUB + shift
-                        parts.append(padded[pl.ds(start, SUB), :])
+                        offset = (comp * TIME + t) * levels * PITCH + LEAD + shift
+                        parts.append(padded[pl.ds(base + offset, SUB), :])
                     return jnp.concatenate(parts, axis=0)
 
                 d_lon.append((rows(1) - rows(-1)) * along)
@@ -200,9 +209,13 @@
             div_at = pl.ds(pl.multiple_of((step + levels * groups) * LANES, LANES), LANES)
             x_buf[here, vort_at] = (d_lon[1] - d_lat[0]).astype(BF16)
             x_buf[here, div_at] = (d_lon[0] + d_lat[1]).astype(BF16)
-        return carry
-
-    lax.fori_loop(0, levels * groups, one_group, 0)
+
+    @pl.loop(0, levels)
+    def _(level):
+        @pl.loop(0, groups)
+        def _(group):
+            one_group(level, group)
+
     store = pltpu.make_async_copy(x_buf, x_out, out_sem)
     store.start()
 
@@ -255,20 +268,35 @@
     square = jnp.concatenate(
         [total] + [pltpu.roll(total, LANES - a * TIME, 1) for a in range(1, TIME // SUB)], axis=0
     )
-    half = dot(table3[...], jnp.concatenate(split(square, 3), axis=0))
-    full = dot(jnp.concatenate(split(half, 3), axis=0), table_t[...])
+    get_tables.wait()
+    table3 = tables[:ALL, :].astype(BF16)
+    table_aug = tables[ALL:2 * ALL, :]
+    table_t = tables[2 * ALL:, :].astype(BF16)
+    stacked = split(square, 3) + [jnp.zeros((TIME, LANES), BF16)]
+    half = dot(table3, jnp.concatenate(stacked, axis=0))
+    full = dot(jnp.concatenate(split(half, 3), axis=0), table_t)
     full = full[:ALL] + full[ALL:2 * ALL] + full[2 * ALL:]
-    aug = jnp.where(iota((ALL, LANES), 1) < 64, full, table_aug[...])
-    row = iota((COLS, 1), 0)
+    aug = jnp.where(iota((ALL, LANES), 1) < 64, full, table_aug)
+    row = iota((COLS, LANES), 0)
     lane_a = iota((COLS, LANES), 1)
     parts = [aug[:COLS], aug[COLS:]]
-    for k in range(COLS):
-        for f in range(FREQS):
-            a = parts[f]
-            at = f * COLS + k
-            pivot = a[k:k + 1, :]
-            scale = jnp.where(row > k, a[:, at:at + 1] / pivot[:, at:at + 1], 0.0)
-            parts[f] = a - scale * pivot
+    panel = 8
+    for start in range(0, COLS, panel):
+        columns = [
+            [
+                jnp.broadcast_to(parts[f][:, at:at + 1], (COLS, LANES))
+                for at in range(f * COLS + start, f * COLS + start + panel)
+            ]
+            for f in range(FREQS)
+        ]
+        for j in range(panel):
+            k = start + j
+            for f in range(FREQS):
+                cols = columns[f]
+                scale = jnp.where(row > k, cols[j] * (1.0 / cols[j][k:k + 1, :]), 0.0)
+                for i in range(j + 1, panel):
+                    cols[i] = cols[i] - scale * cols[i][k:k + 1, :]
+                parts[f] = parts[f] - scale * parts[f][k:k + 1, :]
     rows_done = []
     for f in range(FREQS):
         on_diag = lane_a == iota((COLS, LANES), 0) + f * COLS
@@ -290,15 +318,41 @@
     store.wait()
 
 
-def basis_kernel(mix, x, out):
-    lon_cells = out.shape[2]
-    weights = mix[...]
-    for g in range(0, lon_cells // SUB, 2):
-        part = x[:, g * LANES:(g + 2) * LANES]
-        res = dot(weights, jnp.concatenate([part, part], axis=0))
-        for h in range(2):
-            cols = res[:, h * LANES:(h + 1) * LANES].reshape(ALL, SUB, LANES)
-            out[:, 0, (g + h) * SUB:(g + h + 1) * SUB, :] = cols
+def basis_kernel(mix, x, out, mix_buf, x_buf, out_buf, mix_sem, x_sem, out_sem):
+    slabs, lon_cells = out.shape[1], out.shape[2]
+    width = lon_cells // SUB * LANES
+    pairs = lon_cells // (2 * SUB)
+    get_mix = pltpu.make_async_copy(mix, mix_buf, mix_sem)
+    get_mix.start()
+
+    def get_x(i):
+        part = pl.ds(pl.multiple_of(i * width, LANES), width)
+        return pltpu.make_async_copy(x.at[:, part], x_buf.at[:, part], x_sem.at[i])
+
+    def put(i, g):
+        part = (slice(None), i, pl.ds(g * 2 * SUB, 2 * SUB))
+        return pltpu.make_async_copy(out_buf.at[part], out.at[part], out_sem.at[i, g])
+
+    for i in range(slabs):
+        get_x(i).start()
+    get_mix.wait()
+
+    @pl.loop(0, slabs)
+    def _(i):
+        get_x(i).wait()
+        for g in range(pairs):
+            at = pl.multiple_of(i * width + g * 2 * LANES, LANES)
+            part = x_buf[:, pl.ds(at, 2 * LANES)]
+            res = dot(mix_buf[...], jnp.concatenate([part, part], axis=0))
+            for h in range(2):
+                cols = res[:, h * LANES:(h + 1) * LANES].reshape(ALL, SUB, LANES)
+                out_buf[:, i, (2 * g + h) * SUB:(2 * g + h + 1) * SUB, :] = cols
+            put(i, g).start()
+
+    @pl.loop(0, slabs)
+    def _(i):
+        for g in range(pairs):
+            put(i, g).wait()
 
 
 def body(n_lon, n_lat, winds):
@@ -306,16 +360,19 @@
     cells = levels * lon_cells
     columns = 2 * cells // SUB * LANES
     side = TIME * SUB
-    table = taper_table()
-    table3 = np.concatenate([table] * 3, axis=1)
-    table_t = np.zeros((LANES, LANES), ml_dtypes.bfloat16)
-    table_t[:TIME, :ALL] = table.T
-    table_aug = np.zeros((ALL, LANES), np.float32)
-    table_aug[:, 64:64 + TIME] = table.astype(np.float32)
+    table = taper_table().astype(np.float32)
+    used = n_lat * 3 * SUB + 2 * ALL + LANES
+    consts = np.zeros((8192, LANES), np.float32)
     coef = lat_coefficients(n_lon * lon_cells, n_lat * lat_cells, n_lat)
+    consts[:n_lat * 3 * SUB] = coef.reshape(-1, LANES)
+    tables = consts[n_lat * 3 * SUB:used]
+    tables[:ALL, :3 * TIME] = np.concatenate([table] * 3, axis=1)
+    tables[ALL:2 * ALL, 64:64 + TIME] = table
+    tables[2 * ALL:2 * ALL + TIME, :ALL] = table.T
     rows_total = 2 * levels * lon_cells * n_lon * lat_cells * n_lat
     vmem = pl.BlockSpec(memory_space=pltpu.VMEM)
     anywhere = pl.BlockSpec(memory_space=pl.ANY)
+    hbm = pl.BlockSpec(memory_space=pltpu.HBM)
     blocks = 2 * TIME * levels
     dma = pltpu.SemaphoreType.DMA
     x, mix = pl.pallas_call(
@@ -324,11 +381,13 @@
             jax.ShapeDtypeStruct((side, columns), BF16),
             jax.ShapeDtypeStruct((ALL * SUB, 2 * side), BF16),
         ),
-        in_specs=[anywhere, vmem, vmem, vmem, vmem],
+        in_specs=[hbm, hbm],
         out_specs=(anywhere, vmem),
         scratch_shapes=[
+            pltpu.VMEM((3 * SUB, LANES), F32),
+            pltpu.VMEM((2 * ALL + LANES, LANES), F32),
             pltpu.VMEM((2 * TIME, cells, LANES), BF16),
-            pltpu.VMEM((blocks * PITCH, LANES), F32),
+            pltpu.VMEM((blocks * PITCH + LEAD, LANES), F32),
             pltpu.VMEM((side, columns), BF16),
             pltpu.VMEM((cells, LANES), BF16),
             pltpu.VMEM((cells, LANES), BF16),
@@ -344,6 +403,7 @@
             pltpu.VMEM((SUB, LANES), F32),
             pltpu.VMEM((n_lat - 1, SUB, LANES), F32),
             dma((CHUNKS,)),
+            dma((2,)),
             dma(()),
             dma((4,)),
             dma((4,)),
@@ -353,27 +413,27 @@
             dma((n_lat - 1,)),
         ],
         compiler_params=pltpu.CompilerParams(
-            collective_id=0, has_side_effects=True, vmem_limit_bytes=40 * 2**20
+            collective_id=0, has_side_effects=True, vmem_limit_bytes=50 * 2**20
         ),
         name="fields",
     )(
         winds.reshape(2 * TIME, cells, LANES),
-        jnp.asarray(coef),
-        jnp.asarray(table3),
-        jnp.asarray(table_t),
-        jnp.asarray(table_aug),
-    )
-    width = lon_cells // SUB * LANES
+        jnp.asarray(consts),
+    )
     basis = pl.pallas_call(
         basis_kernel,
-        grid=(2 * levels,),
         out_shape=jax.ShapeDtypeStruct((ALL, 2 * levels, lon_cells, LANES), F32),
-        in_specs=[
-            pl.BlockSpec((ALL * SUB, 2 * side), lambda i: (0, 0)),
-            pl.BlockSpec((side, width), lambda i: (0, i)),
+        in_specs=[anywhere, anywhere],
+        out_specs=hbm,
+        scratch_shapes=[
+            pltpu.VMEM((ALL * SUB, 2 * side), BF16),
+            pltpu.VMEM((side, columns), BF16),
+            pltpu.VMEM((ALL, 2 * levels, lon_cells, LANES), F32),
+            dma(()),
+            dma((2 * levels,)),
+            dma((2 * levels, lon_cells // (2 * SUB))),
         ],
-        out_specs=pl.BlockSpec((ALL, 1, lon_cells, LANES), lambda i: (0, i, 0, 0)),
-        compiler_params=pltpu.CompilerParams(vmem_limit_bytes=40 * 2**20),
+        compiler_params=pltpu.CompilerParams(vmem_limit_bytes=20 * 2**20),
         name="basis",
     )(mix, x)
     return basis.reshape(ALL, 2, levels, lon_cells, lat_cells)

time: 43.4 us -> 36.8 us (0.85)
  local copies, waits for them, and re-layouts: 4.89 us -> 0 us
  Pallas kernels: 38.1 us -> 36.6 us
    unnamed x10 -> x0, local copies, waits for them, and re-layouts: 4.89 us -> none
    pallas_call x1, Pallas kernels: 31.5 us -> 30.7 us  [body(): pl.pallas_call(functools.partial(fields_kernel, n_lon, n_lat, levels, lon...]
    pallas_call x1, Pallas kernels: 6.59 us -> 5.93 us  [body(): pl.pallas_call(basis_kernel, out_shape=jax.ShapeDtypeStruct((ALL, 2 * lev...]
where the time goes in v2:
time: 36.8 us; the launch traced here: 36.6 us
  Pallas kernels  36.6 us (99%)
    pallas_call x1, Pallas kernels, body(): pl.pallas_call(functools.partial(fields_kernel, n_lon, n_lat, levels, lon...  30.7 us
    pallas_call x1, Pallas kernels, body(): pl.pallas_call(basis_kernel, out_shape=jax.ShapeDtypeStruct((ALL, 2 * lev...  5.93 us

profile of v2, /device:TPU:0, one launch (start us, length us, event | category | flops | bytes accessed | tf_op | source)
XLA Modules:
  0.0 36.6 jit_solution(6352267636635606913)
XLA Ops:
  0.0 30.7 %fields.1 = (bf16[256,6144]{1,0:T(8,128)(2,1)S(1)}, bf16[384,512]{1,0:T(8,128)(2,1)S(1)}) custom-call(bf16[64,192,128]{2,1,0:T(8,128)(2,1)} %bitcast.2, f32[8192,128]{1,0:T(8,128)} %constant.2.clone.consts), custom_call_target="tpu_custom_call" | custom-call | tf_op jit(solution)/shard_map/fields/pallas_call | solution.py:378
  30.7 5.9 %basis.1 = f32[48,8,48,128]{3,2,1,0:T(8,128)} custom-call(bf16[384,512]{1,0:T(8,128)(2,1)S(1)} %get-tuple-element.7.mix, bf16[256,6144]{1,0:T(8,128)(2,1)S(1)} %get-tuple-element.8.x), custom_call_target="tpu_custom_call" | custom-call | tf_op jit(solution)/shard_map/basis/pallas_call | solution.py:423

commit v3 on v2

--- a/solution.py
+++ b/solution.py
@@ -128,7 +128,7 @@
     packed = jnp.zeros((cells // SUB, SUB, LANES), F32)
     for c in range(CHUNKS):
         load(c).wait()
-        packed = lax.fori_loop(c * per, (c + 1) * per, widen, packed)
+        packed = lax.fori_loop(c * per, (c + 1) * per, widen, packed, unroll=8)
     pbuf[...] = packed.reshape(cells, LANES).astype(BF16)
 
     pl.semaphore_wait(barrier, n_lon + n_lat - 2)
@@ -164,11 +164,6 @@
         from_left[...].astype(F32),
         pltpu.roll(from_right[...].astype(F32), LANES - 2, 1),
     )
-    east.wait_recv()
-    padded[pl.ds(LEAD - 1, blocks, stride=PITCH), :] = row_prev[...].astype(F32)
-    west.wait_recv()
-    padded[pl.ds(LEAD + lon_cells, blocks, stride=PITCH), :] = row_next[...].astype(F32)
-
     batch = 4
     lane = iota((batch * SUB, LANES), 1)
     first = lane == 0
@@ -180,7 +175,7 @@
 
     def one_group(level, group):
         step = level * groups + group
-        base = level * PITCH + group * SUB
+        base = pl.multiple_of(level * PITCH + group * SUB, SUB)
         edge = edges[pl.ds(pl.multiple_of(step * SUB, SUB), SUB), :]
         for t0 in range(0, TIME, batch):
             d_lon, d_lat = [], []
@@ -212,9 +207,24 @@
 
     @pl.loop(0, levels)
     def _(level):
-        @pl.loop(0, groups)
-        def _(group):
+        def inner(group, carry):
             one_group(level, group)
+            return carry
+
+        lax.fori_loop(1, groups - 1, inner, 0, unroll=2)
+
+    east.wait_recv()
+    padded[pl.ds(LEAD - 1, blocks, stride=PITCH), :] = row_prev[...].astype(F32)
+    west.wait_recv()
+    padded[pl.ds(LEAD + lon_cells, blocks, stride=PITCH), :] = row_next[...].astype(F32)
+
+    @pl.loop(0, levels)
+    def _(level):
+        def outer(end, carry):
+            one_group(level, end * (groups - 1))
+            return carry
+
+        lax.fori_loop(0, 2, outer, 0, unroll=2)
 
     store = pltpu.make_async_copy(x_buf, x_out, out_sem)
     store.start()

time: 36.8 us -> 32.2 us (0.88)
  Pallas kernels: 36.6 us -> 32.1 us
    pallas_call x1, Pallas kernels: 30.7 us -> 26.1 us  [body(): pl.pallas_call(functools.partial(fields_kernel, n_lon, n_lat, levels, lon...]
where the time goes in v3:
time: 32.2 us; the launch traced here: 32.1 us
  Pallas kernels  32.1 us (100%)
    pallas_call x1, Pallas kernels, body(): pl.pallas_call(functools.partial(fields_kernel, n_lon, n_lat, levels, lon...  26.1 us
    pallas_call x1, Pallas kernels, body(): pl.pallas_call(basis_kernel, out_shape=jax.ShapeDtypeStruct((ALL, 2 * lev...  5.93 us

profile of v3, /device:TPU:0, one launch (start us, length us, event | category | flops | bytes accessed | tf_op | source)
XLA Modules:
  0.0 32.1 jit_solution(2853781666847679686)
XLA Ops:
  0.0 26.1 %fields.1 = (bf16[256,6144]{1,0:T(8,128)(2,1)S(1)}, bf16[384,512]{1,0:T(8,128)(2,1)S(1)}) custom-call(bf16[64,192,128]{2,1,0:T(8,128)(2,1)} %bitcast.2, f32[8192,128]{1,0:T(8,128)} %constant.2.clone.consts), custom_call_target="tpu_custom_call" | custom-call | tf_op jit(solution)/shard_map/fields/pallas_call | solution.py:388
  26.1 5.9 %basis.1 = f32[48,8,48,128]{3,2,1,0:T(8,128)} custom-call(bf16[384,512]{1,0:T(8,128)(2,1)S(1)} %get-tuple-element.7.mix, bf16[256,6144]{1,0:T(8,128)(2,1)S(1)} %get-tuple-element.8.x), custom_call_target="tpu_custom_call" | custom-call | tf_op jit(solution)/shard_map/basis/pallas_call | solution.py:433

commit v4 on v3

--- a/solution.py
+++ b/solution.py
@@ -16,6 +16,7 @@
 COLS = 2 * TAPERS
 ALL = FREQS * COLS
 SUB = 8
+HALF = 4
 LANES = 128
 PITCH = 56
 LEAD = 8
@@ -173,10 +174,16 @@
         jnp.concatenate([coef[i * SUB:(i + 1) * SUB, :]] * batch, axis=0) for i in range(3)
     )
 
+    low = (iota((SUB, LANES), 0) < HALF)[None]
+
+    def column(slab, group, h):
+        pair = slab * (groups // 2) + group // 2
+        at = (pair * 2 + h) * 2 + lax.rem(group, 2)
+        return pl.ds(pl.multiple_of(at * LANES, LANES), LANES)
+
     def one_group(level, group):
-        step = level * groups + group
         base = pl.multiple_of(level * PITCH + group * SUB, SUB)
-        edge = edges[pl.ds(pl.multiple_of(step * SUB, SUB), SUB), :]
+        edge = edges[pl.ds(pl.multiple_of(level * lon_cells + group * SUB, SUB), SUB), :]
         for t0 in range(0, TIME, batch):
             d_lon, d_lat = [], []
             for comp in range(2):
@@ -199,11 +206,22 @@
                 nxt = jnp.where(last, halo, pltpu.roll(center, LANES - 1, 1))
                 prv = jnp.where(first, halo, pltpu.roll(center, 1, 1))
                 d_lat.append(nxt * ahead - prv * behind)
-            here = pl.ds(t0 * SUB, batch * SUB)
-            vort_at = pl.ds(pl.multiple_of(step * LANES, LANES), LANES)
-            div_at = pl.ds(pl.multiple_of((step + levels * groups) * LANES, LANES), LANES)
-            x_buf[here, vort_at] = (d_lon[1] - d_lat[0]).astype(BF16)
-            x_buf[here, div_at] = (d_lon[0] + d_lat[1]).astype(BF16)
+            for slab, field in ((0, d_lon[1] - d_lat[0]), (levels, d_lon[0] + d_lat[1])):
+                by_t = field.reshape(batch // 2, 2, SUB, LANES)
+                even, odd = by_t[:, 0], by_t[:, 1]
+                crossed = pltpu.roll(jnp.where(low, odd, even), HALF, 1)
+                halves = (jnp.where(low, even, crossed), jnp.where(low, crossed, odd))
+                for h in range(2):
+                    x_buf[pl.ds(t0 * HALF, batch * HALF), column(slab + level, group, h)] = (
+                        halves[h].reshape(batch * HALF, LANES).astype(BF16)
+                    )
+        x = jnp.concatenate(
+            [x_buf[:, column(slab + level, group, h)] for slab in (0, levels) for h in range(2)],
+            axis=1,
+        )
+        gram[...] += lax.dot_general(x, x, (((1,), (1,)), ((), ())), preferred_element_type=F32)
+
+    gram[...] = jnp.zeros_like(gram)
 
     @pl.loop(0, levels)
     def _(level):
@@ -229,20 +247,14 @@
     store = pltpu.make_async_copy(x_buf, x_out, out_sem)
     store.start()
 
-    wide = 8 * LANES
-    side = TIME * SUB
-
-    def add_gram(c, carry):
-        x = x_buf[:, pl.ds(pl.multiple_of(c * wide, wide), wide)]
-        term = lax.dot_general(x, x, (((1,), (1,)), ((), ())), preferred_element_type=F32)
-        gram[...] = gram[...] + term
-        return carry
-
-    gram[...] = jnp.zeros_like(gram)
-    lax.fori_loop(0, 2 * levels * groups * LANES // wide, add_gram, 0)
-    same = iota((side, side), 0) % SUB == iota((side, side), 1) % SUB
-    by_time = jnp.sum(jnp.where(same, gram[...], 0.0).reshape(TIME, SUB, side), axis=1)
-    fold = (iota((side, LANES), 0) // SUB == iota((side, LANES), 1)).astype(F32).astype(BF16)
+    side = TIME * HALF
+    same = iota((side, side), 0) % HALF == iota((side, side), 1) % HALF
+    fold = (iota((side, LANES), 0) // HALF == iota((side, LANES), 1)).astype(F32).astype(BF16)
+    fold_t = (iota((TIME, side), 0) == iota((TIME, side), 1) // HALF).astype(F32).astype(BF16)
+    masked = jnp.where(same, gram[...], 0.0)
+    by_time = dot(
+        jnp.concatenate([fold_t] * 3, axis=1), jnp.concatenate(split(masked, 3), axis=0)
+    )
     folded = dot(jnp.concatenate(split(by_time, 3), axis=0), fold)
     times = folded[:TIME] + folded[TIME:2 * TIME] + folded[2 * TIME:]
     tile = times[:SUB]
@@ -313,13 +325,16 @@
         diag = jnp.sum(jnp.where(on_diag, parts[f], 0.0), axis=1, keepdims=True)
         rows_done.append(parts[f] / jnp.sqrt(diag))
     mix = jnp.concatenate(rows_done, axis=0)
-    spread = (iota((LANES, side), 0) - 64 == iota((LANES, side), 1) // SUB).astype(F32).astype(BF16)
-    wide_mix = dot(jnp.concatenate(split(mix, 2), axis=0), spread)
-    tall = jnp.broadcast_to(wide_mix[:, None, :], (2 * ALL, SUB, side)).reshape(2 * ALL * SUB, side)
-    keep = iota(tall.shape, 0) % SUB == iota(tall.shape, 1) % SUB
-    tall = jnp.where(keep, tall, 0.0).astype(BF16)
-    mix_out[:, :side] = tall[:ALL * SUB]
-    mix_out[:, side:] = tall[ALL * SUB:]
+    spread = (iota((LANES, side), 0) - 64 == iota((LANES, side), 1) // HALF).astype(F32).astype(BF16)
+    parts = dot(jnp.concatenate(split(mix, 2), axis=0), spread).astype(BF16)
+    wide_mix = jnp.concatenate([parts[:ALL], parts[ALL:]], axis=1)
+    tall = ALL * HALF
+    r = iota((2 * tall, ALL), 0)
+    source = jnp.where(r < tall, r >> 2, ((r - tall) >> 2) ^ 1)
+    pick = (source == iota((2 * tall, ALL), 1)).astype(F32).astype(BF16)
+    spread_rows = dot(pick, wide_mix)
+    keep = iota((2 * tall, 2 * side), 0) % HALF == iota((2 * tall, 2 * side), 1) % HALF
+    mix_out[...] = jnp.where(keep, spread_rows, 0.0).astype(BF16)
 
     pl.when(lat < n_lat - 1)(lambda: up.wait_send())
     pl.when(lat > 0)(lambda: down.wait_send())
@@ -329,9 +344,11 @@
 
 
 def basis_kernel(mix, x, out, mix_buf, x_buf, out_buf, mix_sem, x_sem, out_sem):
-    slabs, lon_cells = out.shape[1], out.shape[2]
-    width = lon_cells // SUB * LANES
+    slabs, lon_cells = out.shape[2], out.shape[3]
+    width = lon_cells // HALF * LANES
     pairs = lon_cells // (2 * SUB)
+    tall = ALL * HALF
+    low = (iota((SUB, LANES), 0) < HALF)[None]
     get_mix = pltpu.make_async_copy(mix, mix_buf, mix_sem)
     get_mix.start()
 
@@ -340,7 +357,7 @@
         return pltpu.make_async_copy(x.at[:, part], x_buf.at[:, part], x_sem.at[i])
 
     def put(i, g):
-        part = (slice(None), i, pl.ds(g * 2 * SUB, 2 * SUB))
+        part = (slice(None), slice(None), i, pl.ds(g * 2 * SUB, 2 * SUB))
         return pltpu.make_async_copy(out_buf.at[part], out.at[part], out_sem.at[i, g])
 
     for i in range(slabs):
@@ -351,12 +368,19 @@
     def _(i):
         get_x(i).wait()
         for g in range(pairs):
-            at = pl.multiple_of(i * width + g * 2 * LANES, LANES)
-            part = x_buf[:, pl.ds(at, 2 * LANES)]
-            res = dot(mix_buf[...], jnp.concatenate([part, part], axis=0))
+            res = []
             for h in range(2):
-                cols = res[:, h * LANES:(h + 1) * LANES].reshape(ALL, SUB, LANES)
-                out_buf[:, i, (2 * g + h) * SUB:(2 * g + h + 1) * SUB, :] = cols
+                at = pl.multiple_of(i * width + (2 * g + h) * 2 * LANES, LANES)
+                part = x_buf[:, pl.ds(at, 2 * LANES)]
+                rows = mix_buf[h * tall:(h + 1) * tall, :]
+                res.append(dot(rows, jnp.concatenate([part, part], axis=0)))
+            for w in range(2):
+                near, far = (
+                    r[:, w * LANES:(w + 1) * LANES].reshape(ALL // 2, SUB, LANES) for r in res
+                )
+                here = slice((2 * g + w) * SUB, (2 * g + w + 1) * SUB)
+                out_buf[:, 0, i, here, :] = jnp.where(low, near, far)
+                out_buf[:, 1, i, here, :] = pltpu.roll(jnp.where(low, far, near), HALF, 1)
             put(i, g).start()
 
     @pl.loop(0, slabs)
@@ -368,8 +392,8 @@
 def body(n_lon, n_lat, winds):
     _, times, levels, lon_cells, lat_cells = winds.shape
     cells = levels * lon_cells
-    columns = 2 * cells // SUB * LANES
-    side = TIME * SUB
+    columns = 2 * cells // HALF * LANES
+    side = TIME * HALF
     table = taper_table().astype(np.float32)
     used = n_lat * 3 * SUB + 2 * ALL + LANES
     consts = np.zeros((8192, LANES), np.float32)
@@ -389,7 +413,7 @@
         functools.partial(fields_kernel, n_lon, n_lat, levels, lon_cells, rows_total),
         out_shape=(
             jax.ShapeDtypeStruct((side, columns), BF16),
-            jax.ShapeDtypeStruct((ALL * SUB, 2 * side), BF16),
+            jax.ShapeDtypeStruct((2 * ALL * HALF, 2 * side), BF16),
         ),
         in_specs=[hbm, hbm],
         out_specs=(anywhere, vmem),
@@ -432,13 +456,13 @@
     )
     basis = pl.pallas_call(
         basis_kernel,
-        out_shape=jax.ShapeDtypeStruct((ALL, 2 * levels, lon_cells, LANES), F32),
+        out_shape=jax.ShapeDtypeStruct((ALL // 2, 2, 2 * levels, lon_cells, LANES), F32),
         in_specs=[anywhere, anywhere],
         out_specs=hbm,
         scratch_shapes=[
-            pltpu.VMEM((ALL * SUB, 2 * side), BF16),
+            pltpu.VMEM((2 * ALL * HALF, 2 * side), BF16),
             pltpu.VMEM((side, columns), BF16),
-            pltpu.VMEM((ALL, 2 * levels, lon_cells, LANES), F32),
+            pltpu.VMEM((ALL // 2, 2, 2 * levels, lon_cells, LANES), F32),
             dma(()),
             dma((2 * levels,)),
             dma((2 * levels, lon_cells // (2 * SUB))),

time: 32.2 us -> 32 us (level)
    pallas_call x1, Pallas kernels: 5.93 us -> 4.7 us  [body(): pl.pallas_call(basis_kernel, out_shape=jax.ShapeDtypeStruct((ALL // 2, 2,...]
    pallas_call x1, Pallas kernels: 26.1 us -> 27.2 us  [body(): pl.pallas_call(functools.partial(fields_kernel, n_lon, n_lat, levels, lon...]
where the time goes in v4:
time: 32 us; the launch traced here: 31.9 us
  Pallas kernels  31.9 us (100%)
    pallas_call x1, Pallas kernels, body(): pl.pallas_call(functools.partial(fields_kernel, n_lon, n_lat, levels, lon...  27.2 us
    pallas_call x1, Pallas kernels, body(): pl.pallas_call(basis_kernel, out_shape=jax.ShapeDtypeStruct((ALL // 2, 2,...  4.7 us

profile of v4, /device:TPU:0, one launch (start us, length us, event | category | flops | bytes accessed | tf_op | source)
XLA Modules:
  0.0 31.9 jit_solution(13547738523493407086)
XLA Ops:
  0.0 27.2 %fields.1 = (bf16[128,12288]{1,0:T(8,128)(2,1)S(1)}, bf16[384,256]{1,0:T(8,128)(2,1)S(1)}) custom-call(bf16[64,192,128]{2,1,0:T(8,128)(2,1)} %bitcast.2, f32[8192,128]{1,0:T(8,128)} %constant.2.clone.consts), custom_call_target="tpu_custom_call" | custom-call | tf_op jit(solution)/shard_map/fields/pallas_call | solution.py:412
  27.2 4.7 %basis.1 = f32[24,2,8,48,128]{4,3,2,1,0:T(8,128)} custom-call(bf16[384,256]{1,0:T(8,128)(2,1)S(1)} %get-tuple-element.7.mix, bf16[128,12288]{1,0:T(8,128)(2,1)S(1)} %get-tuple-element.8.x), custom_call_target="tpu_custom_call" | custom-call | tf_op jit(solution)/shard_map/basis/pallas_call | solution.py:457

commit v5 on v4

--- a/solution.py
+++ b/solution.py
@@ -176,12 +176,23 @@
 
     low = (iota((SUB, LANES), 0) < HALF)[None]
 
+    def add_gram(which):
+        x = jnp.concatenate(
+            [
+                x_buf[:, column(slab + level, group, h)]
+                for level, group in which for slab in (0, levels) for h in range(2)
+            ],
+            axis=1,
+        )
+        gram[...] += lax.dot_general(x, x, (((1,), (1,)), ((), ())), preferred_element_type=F32)
+
     def column(slab, group, h):
         pair = slab * (groups // 2) + group // 2
-        at = (pair * 2 + h) * 2 + lax.rem(group, 2)
-        return pl.ds(pl.multiple_of(at * LANES, LANES), LANES)
-
-    def one_group(level, group):
+        at = (pair * 2 + h) * 2 + group % 2
+        return pl.ds(at * LANES if isinstance(at, int) else pl.multiple_of(at * LANES, LANES), LANES)
+
+    def one_group(level, group, before):
+        add_gram([(level, before)])
         base = pl.multiple_of(level * PITCH + group * SUB, SUB)
         edge = edges[pl.ds(pl.multiple_of(level * lon_cells + group * SUB, SUB), SUB), :]
         for t0 in range(0, TIME, batch):
@@ -215,18 +226,15 @@
                     x_buf[pl.ds(t0 * HALF, batch * HALF), column(slab + level, group, h)] = (
                         halves[h].reshape(batch * HALF, LANES).astype(BF16)
                     )
-        x = jnp.concatenate(
-            [x_buf[:, column(slab + level, group, h)] for slab in (0, levels) for h in range(2)],
-            axis=1,
-        )
-        gram[...] += lax.dot_general(x, x, (((1,), (1,)), ((), ())), preferred_element_type=F32)
-
     gram[...] = jnp.zeros_like(gram)
+    for slab in range(2 * levels):
+        for h in range(2):
+            x_buf[:, column(slab, 0, h)] = jnp.zeros((TIME * HALF, LANES), BF16)
 
     @pl.loop(0, levels)
     def _(level):
         def inner(group, carry):
-            one_group(level, group)
+            one_group(level, group, group - 1)
             return carry
 
         lax.fori_loop(1, groups - 1, inner, 0, unroll=2)
@@ -239,11 +247,12 @@
     @pl.loop(0, levels)
     def _(level):
         def outer(end, carry):
-            one_group(level, end * (groups - 1))
+            one_group(level, end * (groups - 1), (1 - end) * (groups - 2))
             return carry
 
         lax.fori_loop(0, 2, outer, 0, unroll=2)
 
+    add_gram([(level, groups - 1) for level in range(levels)])
     store = pltpu.make_async_copy(x_buf, x_out, out_sem)
     store.start()
 
@@ -269,6 +278,15 @@
     ]
     for copy in lon_copies:
         copy.start()
+    get_tables.wait()
+    table3 = tables[:ALL, :].astype(BF16)
+    table_aug = tables[ALL:2 * ALL, :]
+    table_t = tables[2 * ALL:, :].astype(BF16)
+    spread = (iota((LANES, side), 0) - 64 == iota((LANES, side), 1) // HALF).astype(F32).astype(BF16)
+    tall = ALL * HALF
+    r = iota((2 * tall, ALL), 0)
+    source = jnp.where(r < tall, r >> 2, ((r - tall) >> 2) ^ 1)
+    pick = (source == iota((2 * tall, ALL), 1)).astype(F32).astype(BF16)
     total = mine[...]
     for d, copy in enumerate(lon_copies):
         copy.wait_recv()
@@ -290,10 +308,6 @@
     square = jnp.concatenate(
         [total] + [pltpu.roll(total, LANES - a * TIME, 1) for a in range(1, TIME // SUB)], axis=0
     )
-    get_tables.wait()
-    table3 = tables[:ALL, :].astype(BF16)
-    table_aug = tables[ALL:2 * ALL, :]
-    table_t = tables[2 * ALL:, :].astype(BF16)
     stacked = split(square, 3) + [jnp.zeros((TIME, LANES), BF16)]
     half = dot(table3, jnp.concatenate(stacked, axis=0))
     full = dot(jnp.concatenate(split(half, 3), axis=0), table_t)
@@ -325,15 +339,10 @@
         diag = jnp.sum(jnp.where(on_diag, parts[f], 0.0), axis=1, keepdims=True)
         rows_done.append(parts[f] / jnp.sqrt(diag))
     mix = jnp.concatenate(rows_done, axis=0)
-    spread = (iota((LANES, side), 0) - 64 == iota((LANES, side), 1) // HALF).astype(F32).astype(BF16)
     parts = dot(jnp.concatenate(split(mix, 2), axis=0), spread).astype(BF16)
     wide_mix = jnp.concatenate([parts[:ALL], parts[ALL:]], axis=1)
-    tall = ALL * HALF
-    r = iota((2 * tall, ALL), 0)
-    source = jnp.where(r < tall, r >> 2, ((r - tall) >> 2) ^ 1)
-    pick = (source == iota((2 * tall, ALL), 1)).astype(F32).astype(BF16)
     spread_rows = dot(pick, wide_mix)
-    keep = iota((2 * tall, 2 * side), 0) % HALF == iota((2 * tall, 2 * side), 1) % HALF
+    keep = (iota((2 * tall, 2 * side), 0) & 3) == (iota((2 * tall, 2 * side), 1) & 3)
     mix_out[...] = jnp.where(keep, spread_rows, 0.0).astype(BF16)
 
     pl.when(lat < n_lat - 1)(lambda: up.wait_send())
@@ -343,30 +352,19 @@
     store.wait()
 
 
-def basis_kernel(mix, x, out, mix_buf, x_buf, out_buf, mix_sem, x_sem, out_sem):
+def basis_kernel(mix_buf, x_buf, out, out_buf, out_sem):
     slabs, lon_cells = out.shape[2], out.shape[3]
     width = lon_cells // HALF * LANES
     pairs = lon_cells // (2 * SUB)
     tall = ALL * HALF
     low = (iota((SUB, LANES), 0) < HALF)[None]
-    get_mix = pltpu.make_async_copy(mix, mix_buf, mix_sem)
-    get_mix.start()
-
-    def get_x(i):
-        part = pl.ds(pl.multiple_of(i * width, LANES), width)
-        return pltpu.make_async_copy(x.at[:, part], x_buf.at[:, part], x_sem.at[i])
 
     def put(i, g):
         part = (slice(None), slice(None), i, pl.ds(g * 2 * SUB, 2 * SUB))
         return pltpu.make_async_copy(out_buf.at[part], out.at[part], out_sem.at[i, g])
 
-    for i in range(slabs):
-        get_x(i).start()
-    get_mix.wait()
-
     @pl.loop(0, slabs)
     def _(i):
-        get_x(i).wait()
         for g in range(pairs):
             res = []
             for h in range(2):
@@ -457,14 +455,10 @@
     basis = pl.pallas_call(
         basis_kernel,
         out_shape=jax.ShapeDtypeStruct((ALL // 2, 2, 2 * levels, lon_cells, LANES), F32),
-        in_specs=[anywhere, anywhere],
+        in_specs=[vmem, vmem],
         out_specs=hbm,
         scratch_shapes=[
-            pltpu.VMEM((2 * ALL * HALF, 2 * side), BF16),
-            pltpu.VMEM((side, columns), BF16),
             pltpu.VMEM((ALL // 2, 2, 2 * levels, lon_cells, LANES), F32),
-            dma(()),
-            dma((2 * levels,)),
             dma((2 * levels, lon_cells // (2 * SUB))),
         ],
         compiler_params=pltpu.CompilerParams(vmem_limit_bytes=20 * 2**20),

time: 32 us -> 29.7 us (0.928)
  Pallas kernels: 31.9 us -> 29.5 us
    pallas_call x1, Pallas kernels: 27.2 us -> 25.5 us  [body(): pl.pallas_call(functools.partial(fields_kernel, n_lon, n_lat, levels, lon...]
    pallas_call x1, Pallas kernels: 4.7 us -> 4.02 us  [body(): pl.pallas_call(basis_kernel, out_shape=jax.ShapeDtypeStruct((ALL // 2, 2,...]
where the time goes in v5:
time: 29.7 us; the launch traced here: 29.5 us
  Pallas kernels  29.5 us (99%)
    pallas_call x1, Pallas kernels, body(): pl.pallas_call(functools.partial(fields_kernel, n_lon, n_lat, levels, lon...  25.5 us
    pallas_call x1, Pallas kernels, body(): pl.pallas_call(basis_kernel, out_shape=jax.ShapeDtypeStruct((ALL // 2, 2,...  4.02 us

profile of v5, /device:TPU:0, one launch (start us, length us, event | category | flops | bytes accessed | tf_op | source)
XLA Modules:
  0.0 29.5 jit_solution(5874449270371936776)
XLA Ops:
  0.0 25.5 %fields.1 = (bf16[128,12288]{1,0:T(8,128)(2,1)S(1)}, bf16[384,256]{1,0:T(8,128)(2,1)S(1)}) custom-call(bf16[64,192,128]{2,1,0:T(8,128)(2,1)} %bitcast.2, f32[8192,128]{1,0:T(8,128)} %constant.2.clone.consts), custom_call_target="tpu_custom_call" | custom-call | tf_op jit(solution)/shard_map/fields/pallas_call | solution.py:410
  25.5 4.0 %basis.1 = f32[24,2,8,48,128]{4,3,2,1,0:T(8,128)} custom-call(bf16[384,256]{1,0:T(8,128)(2,1)S(1)} %get-tuple-element.7.mix_buf, bf16[128,12288]{1,0:T(8,128)(2,1)S(1)} %get-tuple-element.8.x_buf), custom_call_target="tpu_custom_call" | custom-call | tf_op jit(solution)/shard_map/basis/pallas_call | solution.py:455

commit v6 on v5

--- a/solution.py
+++ b/solution.py
@@ -21,6 +21,7 @@
 PITCH = 56
 LEAD = 8
 CHUNKS = 4
+BATCH = 4
 MESH = pl.DeviceIdType.MESH
 F32 = jnp.float32
 BF16 = jnp.bfloat16
@@ -78,7 +79,7 @@
     winds, consts,
     x_out, mix_out,
     coef, tables, raw, padded, x_buf, pbuf, from_left, from_right, edges, row_first, row_last,
-    row_prev, row_next, gram, mine, lon_slots, band, lat_slots,
+    row_prev, row_next, kept, gram, mine, lon_slots, band, lat_slots,
     in_sem, const_sem, out_sem, halo_send, halo_recv, lon_send, lon_recv, lat_send, lat_recv,
 ):
     lon = lax.axis_index("lon")
@@ -158,14 +159,7 @@
     east.start()
     west.start()
 
-    pl.when(lat > 0)(lambda: up.wait_recv())
-    pl.when(lat < n_lat - 1)(lambda: down.wait_recv())
-    edges[...] = jnp.where(
-        iota((cells, LANES), 1) % 2 == 0,
-        from_left[...].astype(F32),
-        pltpu.roll(from_right[...].astype(F32), LANES - 2, 1),
-    )
-    batch = 4
+    batch = BATCH
     lane = iota((batch * SUB, LANES), 1)
     first = lane == 0
     last = lane == LANES - 1
@@ -173,6 +167,9 @@
     along, ahead, behind = (
         jnp.concatenate([coef[i * SUB:(i + 1) * SUB, :]] * batch, axis=0) for i in range(3)
     )
+    ahead_in = jnp.where(last, 0.0, ahead)
+    behind_in = jnp.where(first, 0.0, behind)
+    edge_factor = jnp.where(last, ahead, jnp.where(first, -behind, 0.0))
 
     low = (iota((SUB, LANES), 0) < HALF)[None]
 
@@ -191,33 +188,43 @@
         at = (pair * 2 + h) * 2 + group % 2
         return pl.ds(at * LANES if isinstance(at, int) else pl.multiple_of(at * LANES, LANES), LANES)
 
-    def one_group(level, group, before):
+    def without_halo(level, group, t0):
+        base = pl.multiple_of(level * PITCH + group * SUB, SUB)
+        d_lon, d_lat = [], []
+        for comp in range(2):
+            def rows(shift):
+                parts = []
+                for t in range(t0, t0 + batch):
+                    offset = (comp * TIME + t) * levels * PITCH + LEAD + shift
+                    parts.append(padded[pl.ds(base + offset, SUB), :])
+                return jnp.concatenate(parts, axis=0)
+
+            d_lon.append((rows(1) - rows(-1)) * along)
+            center = rows(0)
+            d_lat.append(
+                pltpu.roll(center, LANES - 1, 1) * ahead_in - pltpu.roll(center, 1, 1) * behind_in
+            )
+        return d_lon[1] - d_lat[0], d_lon[0] + d_lat[1]
+
+    def one_group(level, group, before, begun):
         add_gram([(level, before)])
-        base = pl.multiple_of(level * PITCH + group * SUB, SUB)
         edge = edges[pl.ds(pl.multiple_of(level * lon_cells + group * SUB, SUB), SUB), :]
         for t0 in range(0, TIME, batch):
-            d_lon, d_lat = [], []
-            for comp in range(2):
-                def rows(shift):
-                    parts = []
-                    for t in range(t0, t0 + batch):
-                        offset = (comp * TIME + t) * levels * PITCH + LEAD + shift
-                        parts.append(padded[pl.ds(base + offset, SUB), :])
-                    return jnp.concatenate(parts, axis=0)
-
-                d_lon.append((rows(1) - rows(-1)) * along)
-                center = rows(0)
-                halo = jnp.concatenate(
+            halo = [
+                edge_factor * jnp.concatenate(
                     [
                         pltpu.roll(edge, (LANES - 2 * (comp * TIME + t)) % LANES, 1)
                         for t in range(t0, t0 + batch)
                     ],
                     axis=0,
                 )
-                nxt = jnp.where(last, halo, pltpu.roll(center, LANES - 1, 1))
-                prv = jnp.where(first, halo, pltpu.roll(center, 1, 1))
-                d_lat.append(nxt * ahead - prv * behind)
-            for slab, field in ((0, d_lon[1] - d_lat[0]), (levels, d_lon[0] + d_lat[1])):
+                for comp in range(2)
+            ]
+            if begun:
+                vort, div = (kept[f, t0 // batch, level, group] for f in range(2))
+            else:
+                vort, div = without_halo(level, group, t0)
+            for slab, field in ((0, vort - halo[0]), (levels, div + halo[1])):
                 by_t = field.reshape(batch // 2, 2, SUB, LANES)
                 even, odd = by_t[:, 0], by_t[:, 1]
                 crossed = pltpu.roll(jnp.where(low, odd, even), HALF, 1)
@@ -226,6 +233,24 @@
                     x_buf[pl.ds(t0 * HALF, batch * HALF), column(slab + level, group, h)] = (
                         halves[h].reshape(batch * HALF, LANES).astype(BF16)
                     )
+    @pl.loop(0, levels)
+    def _(level):
+        def early(group, carry):
+            for t0 in range(0, TIME, batch):
+                vort, div = without_halo(level, group, t0)
+                kept[0, t0 // batch, level, group] = vort
+                kept[1, t0 // batch, level, group] = div
+            return carry
+
+        lax.fori_loop(1, groups - 1, early, 0, unroll=2)
+
+    pl.when(lat > 0)(lambda: up.wait_recv())
+    pl.when(lat < n_lat - 1)(lambda: down.wait_recv())
+    edges[...] = jnp.where(
+        iota((cells, LANES), 1) % 2 == 0,
+        from_left[...].astype(F32),
+        pltpu.roll(from_right[...].astype(F32), LANES - 2, 1),
+    )
     gram[...] = jnp.zeros_like(gram)
     for slab in range(2 * levels):
         for h in range(2):
@@ -234,7 +259,7 @@
     @pl.loop(0, levels)
     def _(level):
         def inner(group, carry):
-            one_group(level, group, group - 1)
+            one_group(level, group, group - 1, True)
             return carry
 
         lax.fori_loop(1, groups - 1, inner, 0, unroll=2)
@@ -247,7 +272,7 @@
     @pl.loop(0, levels)
     def _(level):
         def outer(end, carry):
-            one_group(level, end * (groups - 1), (1 - end) * (groups - 2))
+            one_group(level, end * (groups - 1), (1 - end) * (groups - 2), False)
             return carry
 
         lax.fori_loop(0, 2, outer, 0, unroll=2)
@@ -329,7 +354,10 @@
             k = start + j
             for f in range(FREQS):
                 cols = columns[f]
-                scale = jnp.where(row > k, cols[j] * (1.0 / cols[j][k:k + 1, :]), 0.0)
+                pivot = cols[j][k:k + 1, :]
+                guess = pl.reciprocal(pivot, approx=True)
+                inverse = guess * (2.0 - pivot * guess)
+                scale = jnp.where(row > k, cols[j] * inverse, 0.0)
                 for i in range(j + 1, panel):
                     cols[i] = cols[i] - scale * cols[i][k:k + 1, :]
                 parts[f] = parts[f] - scale * parts[f][k:k + 1, :]
@@ -429,6 +457,7 @@
             pltpu.VMEM((blocks, LANES), BF16),
             pltpu.VMEM((blocks, LANES), BF16),
             pltpu.VMEM((blocks, LANES), BF16),
+            pltpu.VMEM((2, TIME // BATCH, levels, lon_cells // SUB, BATCH * SUB, LANES), F32),
             pltpu.VMEM((side, side), F32),
             pltpu.VMEM((SUB, LANES), F32),
             pltpu.VMEM((n_lon - 1, SUB, LANES), F32),

time: 29.7 us -> 28.6 us (0.963)
  Pallas kernels: 29.5 us -> 28.5 us
    pallas_call x1, Pallas kernels: 25.5 us -> 24.5 us  [body(): pl.pallas_call(functools.partial(fields_kernel, n_lon, n_lat, levels, lon...]
where the time goes in v6:
time: 28.6 us; the launch traced here: 28.5 us
  Pallas kernels  28.5 us (100%)
    pallas_call x1, Pallas kernels, body(): pl.pallas_call(functools.partial(fields_kernel, n_lon, n_lat, levels, lon...  24.5 us
    pallas_call x1, Pallas kernels, body(): pl.pallas_call(basis_kernel, out_shape=jax.ShapeDtypeStruct((ALL // 2, 2,...  4.03 us

profile of v6, /device:TPU:0, one launch (start us, length us, event | category | flops | bytes accessed | tf_op | source)
XLA Modules:
  0.0 28.5 jit_solution(10679295337173901769)
XLA Ops:
  0.0 24.5 %fields.1 = (bf16[128,12288]{1,0:T(8,128)(2,1)S(1)}, bf16[384,256]{1,0:T(8,128)(2,1)S(1)}) custom-call(bf16[64,192,128]{2,1,0:T(8,128)(2,1)} %bitcast.2, f32[8192,128]{1,0:T(8,128)} %constant.2.clone.consts), custom_call_target="tpu_custom_call" | custom-call | tf_op jit(solution)/shard_map/fields/pallas_call | solution.py:438
  24.5 4.0 %basis.1 = f32[24,2,8,48,128]{4,3,2,1,0:T(8,128)} custom-call(bf16[384,256]{1,0:T(8,128)(2,1)S(1)} %get-tuple-element.7.mix_buf, bf16[128,12288]{1,0:T(8,128)(2,1)S(1)} %get-tuple-element.8.x_buf), custom_call_target="tpu_custom_call" | custom-call | tf_op jit(solution)/shard_map/basis/pallas_call | solution.py:484

commit v7 on v6

--- a/solution.py
+++ b/solution.py
@@ -130,7 +130,7 @@
     packed = jnp.zeros((cells // SUB, SUB, LANES), F32)
     for c in range(CHUNKS):
         load(c).wait()
-        packed = lax.fori_loop(c * per, (c + 1) * per, widen, packed, unroll=8)
+        packed = lax.fori_loop(c * per, (c + 1) * per, widen, packed, unroll=16)
     pbuf[...] = packed.reshape(cells, LANES).astype(BF16)
 
     pl.semaphore_wait(barrier, n_lon + n_lat - 2)
@@ -242,7 +242,7 @@
                 kept[1, t0 // batch, level, group] = div
             return carry
 
-        lax.fori_loop(1, groups - 1, early, 0, unroll=2)
+        lax.fori_loop(1, groups - 1, early, 0, unroll=4)
 
     pl.when(lat > 0)(lambda: up.wait_recv())
     pl.when(lat < n_lat - 1)(lambda: down.wait_recv())
@@ -262,7 +262,7 @@
             one_group(level, group, group - 1, True)
             return carry
 
-        lax.fori_loop(1, groups - 1, inner, 0, unroll=2)
+        lax.fori_loop(1, groups - 1, inner, 0, unroll=4)
 
     east.wait_recv()
     padded[pl.ds(LEAD - 1, blocks, stride=PITCH), :] = row_prev[...].astype(F32)
@@ -391,7 +391,7 @@
         part = (slice(None), slice(None), i, pl.ds(g * 2 * SUB, 2 * SUB))
         return pltpu.make_async_copy(out_buf.at[part], out.at[part], out_sem.at[i, g])
 
-    @pl.loop(0, slabs)
+    @pl.loop(0, slabs, unroll=4)
     def _(i):
         for g in range(pairs):
             res = []
@@ -447,7 +447,7 @@
             pltpu.VMEM((3 * SUB, LANES), F32),
             pltpu.VMEM((2 * ALL + LANES, LANES), F32),
             pltpu.VMEM((2 * TIME, cells, LANES), BF16),
-            pltpu.VMEM((blocks * PITCH + LEAD, LANES), F32),
+            pltpu.VMEM(((blocks + 1) * PITCH + LEAD, LANES), F32),
             pltpu.VMEM((side, columns), BF16),
             pltpu.VMEM((cells, LANES), BF16),
             pltpu.VMEM((cells, LANES), BF16),

time: 28.6 us -> 27.2 us (0.951)
  Pallas kernels: 28.5 us -> 27 us
    pallas_call x1, Pallas kernels: 24.5 us -> 23 us  [body(): pl.pallas_call(functools.partial(fields_kernel, n_lon, n_lat, levels, lon...]
where the time goes in v7:
time: 27.2 us; the launch traced here: 27 us
  Pallas kernels  27 us (99%)
    pallas_call x1, Pallas kernels, body(): pl.pallas_call(functools.partial(fields_kernel, n_lon, n_lat, levels, lon...  23 us
    pallas_call x1, Pallas kernels, body(): pl.pallas_call(basis_kernel, out_shape=jax.ShapeDtypeStruct((ALL // 2, 2,...  4.03 us

profile of v7, /device:TPU:0, one launch (start us, length us, event | category | flops | bytes accessed | tf_op | source)
XLA Modules:
  0.0 27.0 jit_solution(12125993236279597109)
XLA Ops:
  0.0 23.0 %fields.1 = (bf16[128,12288]{1,0:T(8,128)(2,1)S(1)}, bf16[384,256]{1,0:T(8,128)(2,1)S(1)}) custom-call(bf16[64,192,128]{2,1,0:T(8,128)(2,1)} %bitcast.2, f32[8192,128]{1,0:T(8,128)} %constant.2.clone.consts), custom_call_target="tpu_custom_call" | custom-call | tf_op jit(solution)/shard_map/fields/pallas_call | solution.py:438
  23.0 4.0 %basis.1 = f32[24,2,8,48,128]{4,3,2,1,0:T(8,128)} custom-call(bf16[384,256]{1,0:T(8,128)(2,1)S(1)} %get-tuple-element.7.mix_buf, bf16[128,12288]{1,0:T(8,128)(2,1)S(1)} %get-tuple-element.8.x_buf), custom_call_target="tpu_custom_call" | custom-call | tf_op jit(solution)/shard_map/basis/pallas_call | solution.py:484

commit v8 on v7

--- a/solution.py
+++ b/solution.py
@@ -233,7 +233,7 @@
                     x_buf[pl.ds(t0 * HALF, batch * HALF), column(slab + level, group, h)] = (
                         halves[h].reshape(batch * HALF, LANES).astype(BF16)
                     )
-    @pl.loop(0, levels)
+    @pl.loop(0, levels, unroll=2)
     def _(level):
         def early(group, carry):
             for t0 in range(0, TIME, batch):
@@ -256,7 +256,7 @@
         for h in range(2):
             x_buf[:, column(slab, 0, h)] = jnp.zeros((TIME * HALF, LANES), BF16)
 
-    @pl.loop(0, levels)
+    @pl.loop(0, levels, unroll=2)
     def _(level):
         def inner(group, carry):
             one_group(level, group, group - 1, True)
@@ -269,7 +269,7 @@
     west.wait_recv()
     padded[pl.ds(LEAD + lon_cells, blocks, stride=PITCH), :] = row_next[...].astype(F32)
 
-    @pl.loop(0, levels)
+    @pl.loop(0, levels, unroll=2)
     def _(level):
         def outer(end, carry):
             one_group(level, end * (groups - 1), (1 - end) * (groups - 2), False)

time: 27.2 us -> 26.6 us (0.978)
  Pallas kernels: 27 us -> 26.4 us
    pallas_call x1, Pallas kernels: 23 us -> 22.4 us  [body(): pl.pallas_call(functools.partial(fields_kernel, n_lon, n_lat, levels, lon...]
where the time goes in v8:
time: 26.6 us; the launch traced here: 26.5 us
  Pallas kernels  26.4 us (99%)
    pallas_call x1, Pallas kernels, body(): pl.pallas_call(functools.partial(fields_kernel, n_lon, n_lat, levels, lon...  22.4 us
    pallas_call x1, Pallas kernels, body(): pl.pallas_call(basis_kernel, out_shape=jax.ShapeDtypeStruct((ALL // 2, 2,...  4.03 us

profile of v8, /device:TPU:0, one launch (start us, length us, event | category | flops | bytes accessed | tf_op | source)
XLA Modules:
  0.0 26.5 jit_solution(4305534245276686750)
XLA Ops:
  0.0 22.4 %fields.1 = (bf16[128,12288]{1,0:T(8,128)(2,1)S(1)}, bf16[384,256]{1,0:T(8,128)(2,1)S(1)}) custom-call(bf16[64,192,128]{2,1,0:T(8,128)(2,1)} %bitcast.2, f32[8192,128]{1,0:T(8,128)} %constant.2.clone.consts), custom_call_target="tpu_custom_call" | custom-call | tf_op jit(solution)/shard_map/fields/pallas_call | solution.py:438
  22.4 4.0 %basis.1 = f32[24,2,8,48,128]{4,3,2,1,0:T(8,128)} custom-call(bf16[384,256]{1,0:T(8,128)(2,1)S(1)} %get-tuple-element.7.mix_buf, bf16[128,12288]{1,0:T(8,128)(2,1)S(1)} %get-tuple-element.8.x_buf), custom_call_target="tpu_custom_call" | custom-call | tf_op jit(solution)/shard_map/basis/pallas_call | solution.py:484
